TPU v7x, 32 devices: a whole 2x2x4 slice. The times are simulated.
32 devices in a mesh: dp: 16 (over z, y, x), tensor: 2 (over core).
Axes of the slice: x: 2, y: 2, z: 4, core: 2. Of those that a mesh axis runs over, the one named last changes fastest.
Arguments:
- tokens: bfloat16 [8192, 768], P('dp'), may hold values from -6 to 6
- segment_ids: int32 [16, 512], P('dp'), may hold values from 0 to 7, never falling along the last dimension, each value on 1 to 256 neighbouring positions
- expert_ids: int32 [8192, 2], P('dp'), may hold values from 0 to 3, all different within a row
- slot_order: int32 [16, 1024], P('dp'), may hold values from 0 to 1023, each once within a row
- gain_attn: bfloat16 [768], P('dp'), may hold values from 0.5 to 1.5
- qkv_weight: bfloat16 [768, 3, 768], P('dp', None, 'tensor'), may hold values from -0.21875 to 0.21875
- out_weight: bfloat16 [768, 768], P('tensor', 'dp'), may hold values from -0.625 to 0.625
- gain_ffn: bfloat16 [768], P('dp'), may hold values from 0.5 to 1.5
- router_weight: bfloat16 [768, 4], P('dp'), may hold values from -0.15625 to 0.15625
- gate_up: bfloat16 [4, 768, 2, 2048], P(None, 'dp', None, 'tensor'), may hold values from -0.21875 to 0.21875
- down_weight: bfloat16 [4, 2048, 768], P(None, 'tensor', 'dp'), may hold values from -0.25 to 0.25
- shared_gate_up: bfloat16 [768, 2, 2048], P('dp', None, 'tensor'), may hold values from -0.21875 to 0.21875
- shared_down: bfloat16 [2048, 768], P('tensor', 'dp'), may hold values from -0.1875 to 0.1875
- cotangent: bfloat16 [8192, 768], P('dp'), may hold values from -6 to 6
Outputs:
- output: bfloat16 [8192, 768], P('dp')
- grad_tokens: float32 [8192, 768], P('dp')
- grad_gain_attn: float32 [768], P('dp')
- grad_qkv: float32 [768, 3, 768], P('dp', None, 'tensor')
- grad_out: float32 [768, 768], P('tensor', 'dp')
- grad_gain_ffn: float32 [768], P('dp')
- grad_router: float32 [768, 4], P('dp')
- grad_gate_up: float32 [4, 768, 2, 2048], P(None, 'dp', None, 'tensor')
- grad_down: float32 [4, 2048, 768], P(None, 'tensor', 'dp')
- grad_shared_gate_up: float32 [768, 2, 2048], P('dp', None, 'tensor')
- grad_shared_down: float32 [2048, 768], P('tensor', 'dp')
Inputs may be any that keep to these rules, and one draw needn't show every extreme that they name: `segment_ids`: in each row segment numbers never fall; each document has 1 to 256 tokens and one has exactly that many. `expert_ids`: each row names 2 different experts. Each row is a permutation of the 1024 pairs' ranks; pair t * 2 + r of the sequence has rank slot_order[t * 2 + r].
All inputs are finite; a program needn't handle non-finite values.
Results may differ from a plain program's by a relative error of at most 0.015.
Values may be sent and summed in bfloat16 or wider, within the bound.
A program may use at most 192 MiB of HBM per device.

v0:
```python
import functools
import math

import jax
import jax.numpy as jnp
from jax import lax
from jax.experimental import pallas as pl
from jax.experimental.pallas import tpu as pltpu
from jax.sharding import PartitionSpec as P

HD = 64
GROUP = 4
MESH = pl.DeviceIdType.MESH


epsilon = 1e-06


def rms_scale(values):
    return lax.rsqrt(jnp.mean(values * values, axis=-1, keepdims=True) + epsilon)


def rotary(length, head_dim):
    half_dim = head_dim // 2
    position = jnp.arange(length).astype(jnp.float32)[:, None]
    inverse = jnp.exp(
        jnp.arange(half_dim).astype(jnp.float32) * (-2.0 * math.log(10000.0) / head_dim)
    )
    angles = position * inverse[None, :]
    return (jnp.cos(angles)[:, None, :], jnp.sin(angles)[:, None, :])


def rotate(values, cosine, sine):
    half_dim = values.shape[-1] // 2
    first_half = values[..., :half_dim]
    second_half = values[..., half_dim:]
    return jnp.concatenate(
        [first_half * cosine - second_half * sine, second_half * cosine + first_half * sine],
        axis=-1,
    )


def route_slots(pair_ids, rank_order, capacity, experts):
    length = pair_ids.shape[0]
    top_count = pair_ids.shape[1]
    pair_expert = pair_ids.reshape(-1)
    pair_count = pair_expert.shape[0]
    ordered = jnp.zeros((pair_count,), jnp.int32).at[rank_order].set(pair_expert)
    onehot = (ordered[:, None] == jnp.arange(experts, dtype=jnp.int32)[None, :]).astype(jnp.int32)
    running = jnp.cumsum(onehot, axis=0)
    ranked_slot = jnp.sum(running * onehot, axis=1) - 1
    position = ranked_slot[rank_order]
    kept_pair = position < capacity
    slot_index = jnp.where(kept_pair, pair_expert * capacity + position, experts * capacity)
    token_of_pair = jnp.arange(pair_count, dtype=jnp.int32) // top_count
    slot_token = (
        jnp.full((experts * capacity,), length, jnp.int32)
        .at[slot_index]
        .set(token_of_pair, mode="drop")
    )
    return (slot_token, slot_index.reshape(length, top_count), kept_pair.reshape(length, top_count))


def silu_back(both_parts, grad_hidden):
    gate_part = both_parts[..., 0, :]
    up_part = both_parts[..., 1, :]
    sigma = jax.nn.sigmoid(gate_part)
    slope = sigma * (1.0 + gate_part * (1.0 - sigma))
    return jnp.stack(
        [grad_hidden * up_part * slope, grad_hidden * gate_part * sigma], axis=-2
    ).astype(jnp.bfloat16)


def silu_forward(both_parts):
    return (jax.nn.silu(both_parts[..., 0, :]) * both_parts[..., 1, :]).astype(jnp.bfloat16)


def norm_back(grad_norm, values, scale_rows, gain):
    grad_gain = jnp.sum(grad_norm * values * scale_rows, axis=0)
    inner = grad_norm * gain
    grad_values = scale_rows * inner - values * scale_rows**3 * jnp.mean(
        inner * values, axis=-1, keepdims=True
    )
    return (grad_values, grad_gain)


def split_blocks(length):
    block = min(512, length)
    return (block, length // block)


def masked_scores(query_block, keys_all, query_pos, query_seg, segment, scale):
    positions = jnp.arange(keys_all.shape[0])
    scores = (
        jnp.einsum("qhd,khd->hqk", query_block, keys_all, preferred_element_type=jnp.float32)
        * scale
    )
    allowed = (positions[None, :] <= query_pos[:, None]) & (segment[None, :] == query_seg[:, None])
    return jnp.where(allowed[None], scores, -1e30)


def attend_forward(queries, keys_all, values_all, segment, scale):
    length, head_count, head_dim = queries.shape
    block, count_blocks = split_blocks(length)
    positions = jnp.arange(length)

    def one_block(inputs):
        query_block, query_pos, query_seg = inputs
        scores = masked_scores(query_block, keys_all, query_pos, query_seg, segment, scale)
        largest = jnp.max(scores, axis=-1, keepdims=True)
        expo = jnp.exp(scores - largest)
        total = jnp.sum(expo, axis=-1, keepdims=True)
        probs = (expo / total).astype(jnp.bfloat16)
        mixed = jnp.einsum("hqk,khd->qhd", probs, values_all, preferred_element_type=jnp.float32)
        return (mixed.astype(jnp.bfloat16), (largest + jnp.log(total))[..., 0])

    blocks = (
        queries.reshape(count_blocks, block, head_count, head_dim),
        positions.reshape(count_blocks, block),
        segment.reshape(count_blocks, block),
    )
    mixed_all, log_totals = lax.map(one_block, blocks)
    return (mixed_all.reshape(length, head_count * head_dim), log_totals)


def attend_backward(queries, keys_all, values_all, segment, scale, grad_mixed, log_totals):
    length, head_count, head_dim = queries.shape
    block, count_blocks = split_blocks(length)
    positions = jnp.arange(length)

    def one_block(carry, inputs):
        grad_keys, grad_values = carry
        query_block, query_pos, query_seg, grad_block, log_block = inputs
        scores = masked_scores(query_block, keys_all, query_pos, query_seg, segment, scale)
        probs = jnp.exp(scores - log_block[:, :, None])
        grad_probs = jnp.einsum(
            "qhd,khd->hqk", grad_block, values_all, preferred_element_type=jnp.float32
        )
        inner = jnp.sum(probs * grad_probs, axis=-1, keepdims=True)
        grad_scores = (probs * (grad_probs - inner)).astype(jnp.bfloat16)
        grad_query = (
            jnp.einsum("hqk,khd->qhd", grad_scores, keys_all, preferred_element_type=jnp.float32)
            * scale
        )
        grad_keys = (
            grad_keys
            + jnp.einsum(
                "hqk,qhd->khd", grad_scores, query_block, preferred_element_type=jnp.float32
            )
            * scale
        )
        grad_values = grad_values + jnp.einsum(
            "hqk,qhd->khd",
            probs.astype(jnp.bfloat16),
            grad_block,
            preferred_element_type=jnp.float32,
        )
        return ((grad_keys, grad_values), grad_query)

    zeros_kv = jnp.zeros((length, head_count, head_dim), jnp.float32)
    blocks = (
        queries.reshape(count_blocks, block, head_count, head_dim),
        positions.reshape(count_blocks, block),
        segment.reshape(count_blocks, block),
        grad_mixed.reshape(count_blocks, block, head_count, head_dim),
        log_totals,
    )
    (grad_keys, grad_values), grad_queries = lax.scan(one_block, (zeros_kv, zeros_kv), blocks)
    return (grad_queries.reshape(length, head_count, head_dim), grad_keys, grad_values)


def sum_rows(grad, axis, scatter_dimension, tiled):
    part = lax.psum_scatter(
        grad.astype(jnp.bfloat16), axis, scatter_dimension=scatter_dimension, tiled=tiled
    )
    return part.astype(jnp.float32)


def local_plain(
    tokens,
    segment_ids,
    expert_ids,
    slot_order,
    gain_attn,
    qkv_weight,
    out_weight,
    gain_ffn,
    router_weight,
    gate_up,
    down_weight,
    shared_gate_up,
    shared_down,
    cotangent,
):
    g_one, w_qkv, w_out, g_two, w_router, w_gate_up, w_down, s_gate_up, s_down = (
        lax.all_gather(gain_attn, "dp", axis=0, tiled=True),
        lax.all_gather(qkv_weight, "dp", axis=0, tiled=True),
        lax.all_gather(out_weight, "dp", axis=1, tiled=True),
        lax.all_gather(gain_ffn, "dp", axis=0, tiled=True),
        lax.all_gather(router_weight, "dp", axis=0, tiled=True),
        lax.all_gather(gate_up, "dp", axis=1, tiled=True),
        lax.all_gather(down_weight, "dp", axis=2, tiled=True),
        lax.all_gather(shared_gate_up, "dp", axis=0, tiled=True),
        lax.all_gather(shared_down, "dp", axis=1, tiled=True),
    )
    length = tokens.shape[0]
    width = tokens.shape[1]
    experts_count = w_router.shape[1]
    top_count = expert_ids.shape[1]
    capacity = length * top_count // experts_count
    head_dim = HD
    local_heads = w_qkv.shape[2] // head_dim
    scale = head_dim ** (-0.5)
    segment = segment_ids[0]
    slot_token, slot_index, kept_pair = route_slots(
        expert_ids, slot_order[0], capacity, experts_count
    )
    kept_float = kept_pair.astype(jnp.float32)
    slot_valid = slot_token < length
    slot_rows = jnp.minimum(slot_token, length - 1)
    pair_slots = jnp.minimum(slot_index, experts_count * capacity - 1)
    xfull = tokens.astype(jnp.float32)
    rms_one = rms_scale(xfull)
    xn_one = (xfull * rms_one * g_one.astype(jnp.float32)).astype(jnp.bfloat16)
    projected = jnp.einsum("td,dch->tch", xn_one, w_qkv, preferred_element_type=jnp.float32)
    cosine, sine = rotary(length, head_dim)
    queries = rotate(projected[:, 0].reshape(length, local_heads, head_dim), cosine, sine).astype(
        jnp.bfloat16
    )
    keys_all = rotate(projected[:, 1].reshape(length, local_heads, head_dim), cosine, sine).astype(
        jnp.bfloat16
    )
    values_all = projected[:, 2].reshape(length, local_heads, head_dim).astype(jnp.bfloat16)
    mixed, log_totals = attend_forward(queries, keys_all, values_all, segment, scale)
    attn_share = lax.psum_scatter(
        jnp.dot(mixed, w_out, preferred_element_type=jnp.float32),
        "tensor",
        scatter_dimension=1,
        tiled=True,
    )
    attn = lax.all_gather(attn_share, "tensor", axis=1, tiled=True)
    hidden_state = xfull + attn
    rms_two = rms_scale(hidden_state)
    xn_two = (hidden_state * rms_two * g_two.astype(jnp.float32)).astype(jnp.bfloat16)
    logits = jnp.dot(xn_two, w_router, preferred_element_type=jnp.float32)
    probs = jax.nn.softmax(logits, axis=-1)
    gates = jnp.take_along_axis(probs, expert_ids, axis=1) * kept_float
    dispatched = (xn_two[slot_rows] * slot_valid[:, None].astype(jnp.bfloat16)).reshape(
        experts_count, capacity, width
    )
    both_parts = jnp.einsum(
        "ecd,edjf->ecjf", dispatched, w_gate_up, preferred_element_type=jnp.float32
    )
    expert_hidden = silu_forward(both_parts)
    expert_out = jnp.einsum(
        "ecf,efd->ecd", expert_hidden, w_down, preferred_element_type=jnp.float32
    ).reshape(experts_count * capacity, width)
    picked = expert_out[pair_slots]
    moe = jnp.sum(gates[:, :, None] * picked, axis=1)
    shared_both = jnp.einsum("td,djf->tjf", xn_two, s_gate_up, preferred_element_type=jnp.float32)
    shared_hidden = silu_forward(shared_both)
    shared_out = jnp.dot(shared_hidden, s_down, preferred_element_type=jnp.float32)
    ffn_share = lax.psum_scatter(
        (moe + shared_out).astype(jnp.bfloat16), "tensor", scatter_dimension=1, tiled=True
    ).astype(jnp.float32)
    ffn = lax.all_gather(ffn_share.astype(jnp.bfloat16), "tensor", axis=1, tiled=True).astype(
        ffn_share.dtype
    )
    output = (hidden_state + ffn).astype(jnp.bfloat16)
    grad_y = cotangent.astype(jnp.float32)
    grad_shared_hidden = jnp.einsum(
        "td,fd->tf", cotangent, s_down, preferred_element_type=jnp.float32
    )
    grad_s_down = jnp.einsum(
        "tf,td->fd", shared_hidden, cotangent, preferred_element_type=jnp.float32
    )
    grad_shared_both = silu_back(shared_both, grad_shared_hidden)
    grad_s_gate_up = jnp.einsum(
        "td,tjf->djf", xn_two, grad_shared_both, preferred_element_type=jnp.float32
    )
    grad_xn_shared = jnp.einsum(
        "tjf,djf->td", grad_shared_both, s_gate_up, preferred_element_type=jnp.float32
    )
    slot_gate = (
        jnp.zeros((experts_count * capacity,), jnp.float32)
        .at[slot_index.reshape(-1)]
        .set(gates.reshape(-1), mode="drop")
    )
    grad_expert_out = (
        (slot_gate[:, None] * grad_y[slot_rows])
        .astype(jnp.bfloat16)
        .reshape(experts_count, capacity, width)
    )
    grad_gates_part = kept_float * jnp.sum(grad_y[:, None, :] * picked, axis=-1)
    grad_expert_hidden = jnp.einsum(
        "ecd,efd->ecf", grad_expert_out, w_down, preferred_element_type=jnp.float32
    )
    grad_w_down = jnp.einsum(
        "ecf,ecd->efd", expert_hidden, grad_expert_out, preferred_element_type=jnp.float32
    )
    grad_both = silu_back(both_parts, grad_expert_hidden)
    grad_w_gate_up = jnp.einsum(
        "ecd,ecjf->edjf", dispatched, grad_both, preferred_element_type=jnp.float32
    )
    grad_dispatched = jnp.einsum(
        "ecjf,edjf->ecd", grad_both, w_gate_up, preferred_element_type=jnp.float32
    ).reshape(experts_count * capacity, width)
    grad_xn_moe = jnp.sum(kept_float[:, :, None] * grad_dispatched[pair_slots], axis=1)
    grad_xn_part, grad_gates_share = (
        lax.psum_scatter(grad_xn_shared + grad_xn_moe, "tensor", scatter_dimension=1, tiled=True),
        lax.psum_scatter(grad_gates_part, "tensor", scatter_dimension=1, tiled=True),
    )
    grad_xn_sum, grad_gates = (
        lax.all_gather(grad_xn_part, "tensor", axis=1, tiled=True),
        lax.all_gather(grad_gates_share, "tensor", axis=1, tiled=True),
    )
    expert_match = (
        expert_ids[:, :, None] == jnp.arange(experts_count, dtype=jnp.int32)[None, None, :]
    ).astype(jnp.float32)
    grad_probs = jnp.sum(expert_match * grad_gates[:, :, None], axis=1)
    grad_logits = (
        probs * (grad_probs - jnp.sum(probs * grad_probs, axis=-1, keepdims=True))
    ).astype(jnp.bfloat16)
    grad_w_router = jnp.einsum("td,te->de", xn_two, grad_logits, preferred_element_type=jnp.float32)
    grad_xn_two = grad_xn_sum + jnp.einsum(
        "te,de->td", grad_logits, w_router, preferred_element_type=jnp.float32
    )
    grad_norm_two, grad_g_two = norm_back(
        grad_xn_two, hidden_state, rms_two, g_two.astype(jnp.float32)
    )
    grad_hidden = grad_y + grad_norm_two
    grad_attn = grad_hidden.astype(jnp.bfloat16)
    grad_w_out = jnp.einsum("th,td->hd", mixed, grad_attn, preferred_element_type=jnp.float32)
    grad_mixed = jnp.einsum(
        "td,hd->th", grad_attn, w_out, preferred_element_type=jnp.float32
    ).astype(jnp.bfloat16)
    grad_queries, grad_keys, grad_values = attend_backward(
        queries, keys_all, values_all, segment, scale, grad_mixed, log_totals
    )
    grad_projected = (
        jnp.stack(
            [rotate(grad_queries, cosine, -sine), rotate(grad_keys, cosine, -sine), grad_values],
            axis=1,
        )
        .astype(jnp.bfloat16)
        .reshape(length, 3, local_heads * head_dim)
    )
    grad_w_qkv = jnp.einsum(
        "td,tch->dch", xn_one, grad_projected, preferred_element_type=jnp.float32
    )
    grad_xn_share = lax.psum_scatter(
        jnp.einsum("tch,dch->td", grad_projected, w_qkv, preferred_element_type=jnp.float32).astype(
            jnp.bfloat16
        ),
        "tensor",
        scatter_dimension=1,
        tiled=True,
    ).astype(jnp.float32)
    grad_xn_one = lax.all_gather(
        grad_xn_share.astype(jnp.bfloat16), "tensor", axis=1, tiled=True
    ).astype(grad_xn_share.dtype)
    grad_norm_one, grad_g_one = norm_back(grad_xn_one, xfull, rms_one, g_one.astype(jnp.float32))
    grad_tokens = grad_hidden + grad_norm_one
    (
        grad_g_one,
        grad_w_qkv,
        grad_w_out,
        grad_g_two,
        grad_w_router,
        grad_w_gate_up,
        grad_w_down,
        grad_s_gate_up,
        grad_s_down,
    ) = (
        lax.psum_scatter(grad_g_one, "dp", scatter_dimension=0, tiled=True),
        sum_rows(grad_w_qkv, "dp", scatter_dimension=0, tiled=True),
        sum_rows(grad_w_out, "dp", scatter_dimension=1, tiled=True),
        lax.psum_scatter(grad_g_two, "dp", scatter_dimension=0, tiled=True),
        lax.psum_scatter(grad_w_router, "dp", scatter_dimension=0, tiled=True),
        sum_rows(grad_w_gate_up, "dp", scatter_dimension=1, tiled=True),
        sum_rows(grad_w_down, "dp", scatter_dimension=2, tiled=True),
        sum_rows(grad_s_gate_up, "dp", scatter_dimension=0, tiled=True),
        sum_rows(grad_s_down, "dp", scatter_dimension=1, tiled=True),
    )
    return (
        output,
        grad_tokens,
        grad_g_one,
        grad_w_qkv,
        grad_w_out,
        grad_g_two,
        grad_w_router,
        grad_w_gate_up,
        grad_w_down,
        grad_s_gate_up,
        grad_s_down,
    )


class Place:
    def __init__(self, planes):
        d = lax.axis_index("dp")
        self.planes = planes
        self.d, self.c = d, lax.axis_index("tensor")
        self.z, self.p = d // GROUP, lax.rem(d, GROUP)
        bit0, bit1 = lax.rem(self.p, 2), self.p // 2
        flip0, flip1 = 1 - bit0, 1 - bit1
        self.member = [
            self.p,
            flip0 + 2 * bit1,
            bit0 + 2 * flip1,
            flip0 + 2 * flip1,
        ]

    def near(self, j):
        return (self.z * GROUP + self.member[j], self.c)

    def up(self):
        return (self.d + GROUP, self.c)

    def down(self):
        return (self.d - GROUP, self.c)

    def twin(self):
        return (self.d, 1 - self.c)

    def when(self, condition, action):
        pl.when(condition)(action)

    def has_up(self, k=1):
        return self.z + k < self.planes

    def has_down(self, k=1):
        return self.z - k >= 0

    def greet(self):
        barrier = pltpu.get_barrier_semaphore()

        def hello(device):
            pl.semaphore_signal(barrier, inc=1, device_id=device, device_id_type=MESH)

        hello(self.twin())
        for j in range(1, GROUP):
            hello(self.near(j))
        self.when(self.has_up(), lambda: hello(self.up()))
        self.when(self.has_down(), lambda: hello(self.down()))
        line = self.has_up().astype(jnp.int32) + self.has_down().astype(jnp.int32)
        pl.semaphore_wait(barrier, GROUP + line)


def send(source, target, send_sem, recv_sem, device):
    return pltpu.make_async_remote_copy(
        src_ref=source,
        dst_ref=target,
        send_sem=send_sem,
        recv_sem=recv_sem,
        device_id=device,
        device_id_type=MESH,
    )


class Everywhere:
    def __init__(self, at, own, all_blocks, local_sem, recvs, sends):
        self.at, self.own, self.all = at, own, all_blocks
        self.local_sem, self.recvs, self.sends = local_sem, recvs, sends

    def copy(self, block, source, way, device):
        return send(source, self.all.at[block], self.sends.at[way, block], self.recvs.at[block], device)

    def keep(self):
        return pltpu.make_async_copy(self.own, self.all.at[self.at.d], self.local_sem)

    def landed(self, block):
        self.copy(block, self.own, 0, self.at.near(1)).wait_recv()

    def start_line(self):
        at = self.at
        at.when(at.has_up(), lambda: self.copy(at.d, self.own, 0, at.up()).start())
        at.when(at.has_down(), lambda: self.copy(at.d, self.own, 1, at.down()).start())

    def start_plane(self):
        at = self.at
        self.copy(at.d, self.own, 2, at.near(1)).start()
        self.copy(at.d, self.own, 3, at.near(2)).start()
        self.keep().start()

    def pass_on(self, k):
        at = self.at

        def go(plane, more, way, device_of):
            block = plane * GROUP + at.p
            self.landed(block)
            at.when(more, lambda: self.copy(block, self.all.at[block], way, device_of()).start())

        at.when(at.has_down(k), lambda: go(at.z - k, at.has_up(), 0, at.up))
        at.when(at.has_up(k), lambda: go(at.z + k, at.has_down(), 1, at.down))

    def over_plane(self, k):
        at = self.at

        def go(plane):
            block = plane * GROUP + at.p
            self.copy(block, self.all.at[block], 2, at.near(1)).start()
            self.copy(block, self.all.at[block], 3, at.near(2)).start()

        at.when(at.has_down(k), lambda: go(at.z - k))
        at.when(at.has_up(k), lambda: go(at.z + k))

    def spread(self, k):
        self.pass_on(k)
        self.over_plane(k)

    def cross(self, k):
        at = self.at

        def go(plane):
            first = plane * GROUP + at.member[1]
            second = plane * GROUP + at.member[2]
            even = lax.rem(plane, 2) == 0
            self.landed(first)
            at.when(even, lambda: self.copy(first, self.all.at[first], 3, at.near(2)).start())
            self.landed(second)
            at.when(
                jnp.logical_not(even),
                lambda: self.copy(second, self.all.at[second], 2, at.near(1)).start(),
            )

        if k == 0:
            go(at.z)
        else:
            at.when(at.has_down(k), lambda: go(at.z - k))
            at.when(at.has_up(k), lambda: go(at.z + k))

    def diagonal(self):
        for plane in range(self.at.planes):
            self.landed(plane * GROUP + self.at.member[3])
        self.keep().wait()

    def sent(self):
        at = self.at
        for plane in range(at.planes):
            block = plane * GROUP + at.p
            self.copy(block, self.own, 2, at.near(1)).wait_send()
            self.copy(block, self.own, 3, at.near(2)).wait_send()
            if plane % 2 == 0:
                self.copy(plane * GROUP + at.member[1], self.own, 3, at.near(2)).wait_send()
            else:
                self.copy(plane * GROUP + at.member[2], self.own, 2, at.near(1)).wait_send()

            def gone(way, device_of):
                self.copy(block, self.own, way, device_of()).wait_send()

            at.when((at.z >= plane) & at.has_up(), lambda: gone(0, at.up))
            at.when((at.z <= plane) & at.has_down(), lambda: gone(1, at.down))


class Experts:
    def __init__(self, at, own, all_blocks, local_sem, recvs, sends, across_sends):
        self.at, self.own, self.all = at, own, all_blocks
        self.local_sem, self.recvs, self.sends = local_sem, recvs, sends
        self.across_sends = across_sends

    def line(self, block, source, way, device):
        return send(source, self.all.at[block], self.sends.at[way, block], self.recvs.at[block], device)

    def across(self, j):
        at = self.at
        return send(
            self.own.at[at.member[j]],
            self.all.at[at.d],
            self.across_sends.at[j],
            self.recvs.at[at.d],
            at.near(j),
        )

    def keep(self):
        return pltpu.make_async_copy(self.own.at[self.at.p], self.all.at[self.at.d], self.local_sem)

    def start_plane(self):
        for j in range(1, GROUP):
            self.across(j).start()
        self.keep().start()

    def start_line(self):
        at = self.at
        source = self.own.at[at.p]
        at.when(at.has_up(), lambda: self.line(at.d, source, 0, at.up()).start())
        at.when(at.has_down(), lambda: self.line(at.d, source, 1, at.down()).start())

    def landed(self, block):
        self.line(block, self.own.at[0], 0, self.at.near(1)).wait_recv()

    def plane_step(self, j):
        at = self.at
        block = at.z * GROUP + at.member[j]
        source = self.all.at[block]
        self.landed(block)
        at.when(at.has_up(), lambda: self.line(block, source, 0, at.up()).start())
        at.when(at.has_down(), lambda: self.line(block, source, 1, at.down()).start())

    def line_step(self, k, j):
        at = self.at

        def go(plane, more, way, device_of):
            block = plane * GROUP + at.member[j]
            self.landed(block)
            at.when(more, lambda: self.line(block, self.all.at[block], way, device_of()).start())

        at.when(at.has_down(k), lambda: go(at.z - k, at.has_up(), 0, at.up))
        at.when(at.has_up(k), lambda: go(at.z + k, at.has_down(), 1, at.down))

    def ready(self):
        self.keep().wait()

    def own_sent(self):
        at = self.at
        source = self.own.at[at.p]
        for j in range(1, GROUP):
            self.across(j).wait_send()
        at.when(at.has_up(), lambda: self.line(at.d, source, 0, at.up()).wait_send())
        at.when(at.has_down(), lambda: self.line(at.d, source, 1, at.down()).wait_send())

    def rest_sent(self):
        at = self.at
        for plane in range(at.planes):

            def gone(j, way, device_of):
                block = plane * GROUP + at.member[j]
                self.line(block, self.own.at[0], way, device_of()).wait_send()

            for j in range(GROUP):
                up = at.z >= plane if j else at.z > plane
                down = at.z <= plane if j else at.z < plane
                at.when(up & at.has_up(), lambda: gone(j, 0, at.up))
                at.when(down & at.has_down(), lambda: gone(j, 1, at.down))


def dot_nn(a, b):
    return jnp.dot(a, b, preferred_element_type=jnp.float32)


def dot_nt(a, b):
    return lax.dot_general(a, b, (((1,), (1,)), ((), ())), preferred_element_type=jnp.float32)


def dot_tn(a, b):
    return lax.dot_general(a, b, (((0,), (0,)), ((), ())), preferred_element_type=jnp.float32)


def lanes(count=128):
    return lax.broadcasted_iota(jnp.int32, (1, count), 1)


def turn(values, cosine, sine):
    half = HD // 2
    other = jnp.where(
        lax.rem(lanes(), HD) < half,
        -pltpu.roll(values, 2 * HD - half, 1),
        pltpu.roll(values, half, 1),
    )
    return values * cosine + other * sine


def blocks_of(ref, start, stop):
    block = ref[:, :, start:stop]
    return block.reshape(block.shape[0] * block.shape[1], stop - start)


def attention_blocks(length):
    size = length // 2
    return [(i * size, (i + 1) * size) for i in range(2)]


class PlaneSum:
    def __init__(self, at, own, one, two, came, one_sems, two_sems, line_sems):
        self.at, self.own, self.one, self.two, self.came = at, own, one, two, came
        self.one_sems, self.two_sems, self.line_sems = one_sems, two_sems, line_sems

    def one_copy(self, plane, i, even):
        at = self.at
        j = 1 if even else 2
        target = at.member[3] if i else at.member[j]
        return send(
            self.own.at[plane * GROUP + target],
            self.one.at[plane, i],
            self.one_sems.at[0, plane, i],
            self.one_sems.at[1, plane, i],
            at.near(j),
        )

    def two_copy(self, plane, even):
        return send(
            self.one.at[plane, 1],
            self.two.at[plane],
            self.two_sems.at[0, plane],
            self.two_sems.at[1, plane],
            self.at.near(2 if even else 1),
        )

    def by_parity(self, plane, action):
        even = lax.rem(plane, 2) == 0
        self.at.when(even, lambda: action(True))
        self.at.when(jnp.logical_not(even), lambda: action(False))

    def line(self, source, plane, way, here=False):
        at, sems = self.at, self.line_sems
        slot, device = plane, at.up()
        if way:
            slot = jnp.where(plane == (at.z if here else at.z - 1), at.planes, plane)
            device = at.down()
        return send(
            source, self.came.at[slot], sems.at[0, way, plane], sems.at[1, way, plane], device
        )

    def both_ways(self, action, k):
        at = self.at
        if k == 0:
            action(at.z, 0)
            return
        at.when(at.has_up(k), lambda: action(at.z + k, 0))
        at.when(at.has_down(k), lambda: action(at.z - k, 1))

    def start(self, k):
        def go(plane, way):
            def pair(even):
                self.one_copy(plane, 1, even).start()
                self.one_copy(plane, 0, even).start()

            self.by_parity(plane, pair)

        self.both_ways(go, k)

    def middle(self, k):
        f32 = jnp.float32

        def go(plane, way):
            def stage(even):
                at, one = self.at, self.one
                other = plane * GROUP + (at.member[2] if even else at.member[1])
                self.one_copy(plane, 1, even).wait_recv()
                one[plane, 1] = (one[plane, 1].astype(f32) + self.own[other].astype(f32)).astype(
                    one.dtype
                )
                self.two_copy(plane, even).start()

            self.by_parity(plane, stage)

        self.both_ways(go, k)

    def finish_plane(self, plane):
        f32 = jnp.float32

        def stage(even):
            mine = plane * GROUP + self.at.p
            self.one_copy(plane, 0, even).wait_recv()
            self.two_copy(plane, even).wait_recv()
            self.two[plane] = (
                self.two[plane].astype(f32)
                + self.one[plane, 0].astype(f32)
                + self.own[mine].astype(f32)
            ).astype(self.two.dtype)

        self.by_parity(plane, stage)

    def step(self, k):
        f32 = jnp.float32

        def go(plane, way):
            at = self.at
            self.finish_plane(plane)
            behind = at.has_down() if way == 0 else at.has_up()
            held = self.came

            def add():
                self.line(self.two.at[plane], plane, way, True).wait_recv()
                held[plane] = (held[plane].astype(f32) + self.two[plane].astype(f32)).astype(
                    held.dtype
                )
                self.line(held.at[plane], plane, way).start()

            at.when(behind, add)
            at.when(
                jnp.logical_not(behind), lambda: self.line(self.two.at[plane], plane, way).start()
            )

        self.both_ways(go, k)

    def total(self, out):
        at, f32 = self.at, jnp.float32
        z = at.z
        self.finish_plane(z)
        at.when(at.has_down(), lambda: self.line(self.two.at[z], z, 0, True).wait_recv())
        at.when(at.has_up(), lambda: self.line(self.two.at[z], z, 1, True).wait_recv())
        low = jnp.where(at.has_down(), self.came[z].astype(f32), 0.0)
        high = jnp.where(at.has_up(), self.came[at.planes].astype(f32), 0.0)
        out[...] = (self.two[z].astype(f32) + low + high).astype(out.dtype)

    def sent(self):
        at = self.at
        for plane in range(at.planes):
            even = plane % 2 == 0
            self.one_copy(plane, 0, even).wait_send()
            self.one_copy(plane, 1, even).wait_send()
            self.two_copy(plane, even).wait_send()
            at.when(at.z < plane, lambda: self.line(self.two.at[plane], plane, 0).wait_send())
            at.when(at.z > plane, lambda: self.line(self.two.at[plane], plane, 1).wait_send())


class LineSum:
    def __init__(self, at, own, came, out, columns, line_sems, last_sems):
        self.at, self.own, self.came, self.out = at, own, came, out
        self.line_sems, self.last_sems = line_sems, last_sems
        self.columns, self.size = columns, columns[0].stop - columns[0].start

    def hop(self, source, plane, j, way, here=False):
        at = self.at
        block = plane * GROUP + at.member[j]
        if way == 0:
            slot, device = block, at.up()
        else:
            end = at.z if here else at.z - 1
            slot = jnp.where(plane == end, at.planes, plane) * GROUP + at.member[j]
            device = at.down()
        sems = self.line_sems
        return send(
            source, self.came.at[slot], sems.at[0, way, block], sems.at[1, way, block], device
        )

    def start_plane(self, plane):
        at = self.at

        def go(way):
            for j in range(GROUP):
                self.hop(self.own.at[plane * GROUP + at.member[j]], plane, j, way).start()

        at.when(jnp.logical_not(at.has_down()) & (plane != at.z), lambda: go(0))
        at.when(jnp.logical_not(at.has_up()) & (plane != at.z), lambda: go(1))

    def step(self, k, j):
        at, f32 = self.at, jnp.float32

        def go(plane, way):
            block = plane * GROUP + at.member[j]
            self.hop(self.own.at[block], plane, j, way, True).wait_recv()
            self.came[block] = (
                self.came[block].astype(f32) + self.own[block].astype(f32)
            ).astype(self.came.dtype)
            self.hop(self.came.at[block], plane, j, way).start()

        at.when(at.has_up(k) & at.has_down(), lambda: go(at.z + k, 0))
        at.when(at.has_down(k) & at.has_up(), lambda: go(at.z - k, 1))

    def parts(self, j, here=False):
        at, size = self.at, self.size
        source = self.came.at[at.z * GROUP + at.member[j]]
        target = self.out.at[at.member[j] if here else at.p]
        return [
            send(
                source.at[:, i * size : (i + 1) * size],
                target.at[:, self.columns[i]],
                self.last_sems.at[0, j, i],
                self.last_sems.at[1, j, i],
                at.near(j),
            )
            for i in range(len(self.columns))
        ]

    def total(self, j):
        at, f32, out = self.at, jnp.float32, self.out
        block = at.z * GROUP + at.member[j]
        spare = at.planes * GROUP + at.member[j]
        at.when(at.has_down(), lambda: self.hop(self.own.at[block], at.z, j, 0, True).wait_recv())
        at.when(at.has_up(), lambda: self.hop(self.own.at[block], at.z, j, 1, True).wait_recv())
        low = jnp.where(at.has_down(), self.came[block].astype(f32), 0.0)
        high = jnp.where(at.has_up(), self.came[spare].astype(f32), 0.0)
        total = (self.own[block].astype(f32) + low + high).astype(out.dtype)
        if j == 0:
            for i, columns in enumerate(self.columns):
                out[at.p, :, columns] = total[:, i * self.size : (i + 1) * self.size]
        else:
            self.came[block] = total
            for copy in self.parts(j):
                copy.start()

    def arrive(self, j):
        for copy in self.parts(j, True):
            copy.wait_recv()

    def sent(self):
        at = self.at
        for j in range(1, GROUP):
            for copy in self.parts(j):
                copy.wait_send()
        for plane in range(at.planes):

            def gone(way):
                for j in range(GROUP):
                    self.hop(self.own.at[0], plane, j, way).wait_send()

            at.when(at.z < plane, lambda: gone(0))
            at.when(at.z > plane, lambda: gone(1))


def norm_back_rows(grad, values, gain):
    rms = lax.rsqrt(jnp.mean(values * values, axis=-1, keepdims=True) + epsilon)
    grad_gain = jnp.sum(grad * values * rms, axis=0, keepdims=True)
    inner = grad * gain
    grad_values = rms * inner - values * (rms * rms * rms) * jnp.mean(
        inner * values, axis=-1, keepdims=True
    )
    return grad_values, grad_gain


def branch(x_of, dy_of, rows, weights, start, stride, hidden, act, y_acc, dx_acc):
    f32, bf16 = jnp.float32, jnp.bfloat16
    size, count = 256, rows.stop - rows.start
    step = min(count, 256)

    def body(i, carry):
        offset = pl.multiple_of(i * size, size)

        def weight(part):
            first = pl.multiple_of(start + part * stride + offset, size)
            block = weights[:, :, pl.ds(first, size)]
            return block.reshape(block.shape[0] * block.shape[1], size)

        for first in range(0, count, step):
            some = slice(first, first + step)

            def keep(part, values):
                columns = pl.ds(pl.multiple_of(part * hidden + offset, size), size)
                act[rows.start + first : rows.start + first + step, columns] = values

            g, u = dot_nn(x_of(some), weight(0)), dot_nn(x_of(some), weight(1))
            grad = dot_nn(dy_of(some), weight(2))
            sigma = 1.0 / (1.0 + jnp.exp(-g))
            silu = g * sigma
            eh = (silu * u).astype(bf16)
            dg = (grad * u * (sigma * (1.0 + g * (1.0 - sigma)))).astype(bf16)
            du = (grad * silu).astype(bf16)
            keep(0, dg)
            keep(1, du)
            keep(2, eh)
            y_acc[some, :] += dot_nt(eh, weight(2))
            dx_acc[some, :] += dot_nt(dg, weight(0)) + dot_nt(du, weight(1))
        return carry

    lax.fori_loop(0, hidden // size, body, 0)


def weight_grads(plane, planes, count, x_t, dy_t, act, hidden, grads, start, stride):
    width, bf16 = x_t.shape[0], jnp.bfloat16
    rows = width // planes
    features = pl.ds(pl.multiple_of(plane * rows, 16), rows)
    for part in range(3):
        columns = slice(part * hidden, (part + 1) * hidden)
        left = dy_t if part == 2 else x_t
        block = dot_nn(left[features, :count], act[:count, columns]).astype(bf16)
        target = slice(start + part * stride, start + part * stride + hidden)
        grads[pl.ds(plane * GROUP, GROUP), :, target] = block.reshape(
            GROUP, rows // GROUP, hidden
        )


PROBS, PAIRS, LOGS = 2, 8, 16


def layer_kernel(
    planes,
    experts,
    top,
    heads_width,
    x_ref,
    cot_ref,
    facts,
    facts_t,
    waves,
    a_own,
    s_own,
    e_own,
    out_ref,
    gx_ref,
    a_out,
    s_out,
    e_out,
    aw,
    sw,
    ew,
    tok,
    part_one,
    home,
    act,
    x_t,
    dy_t,
    y_acc,
    dx_acc,
    s_dx,
    q_ref,
    k_ref,
    v_ref,
    o_ref,
    xf_ref,
    row_facts,
    ffn_theirs,
    dx_theirs,
    ret,
    a_one,
    a_two,
    a_came,
    s_one,
    s_two,
    s_came,
    e_came,
    local_sem,
    a_recv,
    a_send,
    s_recv,
    s_send,
    e_recv,
    e_send,
    e_across,
    a_one_sems,
    a_two_sems,
    a_line_sems,
    s_one_sems,
    s_two_sems,
    s_line_sems,
    e_line_sems,
    e_last_sems,
    token_sems,
    home_sems,
    share_sems,
    twin_sems,
):
    f32, bf16 = jnp.float32, jnp.bfloat16
    at = Place(planes)
    length, width = x_ref.shape
    capacity = length * top // experts
    half = capacity // 2
    count = experts * half
    hidden, s_hidden = ew.shape[3] // 3, sw.shape[2] // 6
    step = min(length, 256)
    chunks = [slice(i, i + step) for i in range(0, length, step)]
    seg_col, seg_row = facts[:, 2 * top : 2 * top + 1], facts_t[2 * top : 2 * top + 1, :]

    halves = [
        [slice((2 * k + i) * hidden, (2 * k + i + 1) * hidden) for k in range(3)] for i in range(2)
    ]

    attn_in = Everywhere(at, a_own, aw, local_sem.at[0], a_recv, a_send)
    shared_in = Everywhere(at, s_own, sw, local_sem.at[1], s_recv, s_send)
    expert_in = [
        Experts(
            at,
            part_one.at[i, :, : e_own.shape[1]],
            ew.at[i],
            local_sem.at[2 + i],
            e_recv.at[i],
            e_send.at[i],
            e_across.at[i],
        )
        for i in range(2)
    ]
    expert_out = [
        LineSum(
            at, ew.at[i], e_came.at[i], e_out, halves[i], e_line_sems.at[i], e_last_sems.at[i]
        )
        for i in range(2)
    ]
    shared_out = PlaneSum(at, sw, s_one, s_two, s_came, s_one_sems, s_two_sems, s_line_sems)
    attn_out = PlaneSum(at, aw, a_one, a_two, a_came, a_one_sems, a_two_sems, a_line_sems)

    xa_ref = act.at[:length, :width]
    placed = act.at[:, : 2 * width]
    part_mine = act.at[length:, :width]
    part_theirs = ret.at[:length, :width]
    grad_o = act.at[:length, :heads_width]
    dproj = act.at[:length, heads_width : 4 * heads_width]
    bias = y_acc
    dk_acc, dv_acc = (dx_acc.at[:, 128 * i : 128 * (i + 1)] for i in range(2))

    def halve(i, k):
        return pltpu.make_async_copy(
            e_own.at[:, :, halves[i][k]],
            part_one.at[i, :, : e_own.shape[1], k * hidden : (k + 1) * hidden],
            local_sem.at[4 + 3 * i + k],
        )

    for i in range(2):
        for k in range(3):
            halve(i, k).start()
    at.greet()
    attn_in.start_line()
    attn_in.start_plane()
    for k in range(3):
        halve(0, k).wait()
    expert_in[0].start_plane()
    expert_in[0].start_line()
    shared_in.start_line()
    for k in range(3):
        halve(1, k).wait()

    todo = []

    def tick(amount=1):
        for _ in range(amount):
            if todo:
                todo.pop(0)()

    def lines(i, k, members=range(GROUP)):
        return [functools.partial(expert_in[i].line_step, k, j) for j in members]

    def second_half():
        expert_in[1].start_line()
        for j in range(1, GROUP):
            expert_in[1].plane_step(j)

    todo += lines(0, 1)
    todo.append(second_half)
    todo.append(functools.partial(shared_in.pass_on, planes - 1))
    for k in range(2, planes):
        todo += lines(0, k) + lines(1, k - 1)
    todo += lines(1, planes - 1)
    def masks():
        for start, stop in attention_blocks(length):
            row = lax.broadcasted_iota(jnp.int32, (stop - start, stop), 0) + start
            column = lax.broadcasted_iota(jnp.int32, (stop - start, stop), 1)
            allowed = (column <= row) & (seg_col[start:stop, :] == seg_row[:, :stop])
            bias[start:stop, :stop] = jnp.where(allowed, 0.0, -1e30)

    masks()

    def slot_of(expert_id, position):
        which = position // half
        apart = which + at.c - 2 * which * at.c
        bit0, bit1 = lax.rem(expert_id, 2), expert_id // 2
        p0, p1 = lax.rem(at.p, 2), at.p // 2
        distance = (bit0 + p0 - 2 * bit0 * p0) + 2 * (bit1 + p1 - 2 * bit1 * p1)
        slot = apart * count + distance * half + lax.rem(position, half)
        return jnp.where(position < capacity, slot, -1)

    slot_cols, slot_rows = [], []
    for r in range(top):
        ids_col, order_col = facts[:, r : r + 1], facts[:, top + r : top + r + 1]
        ids_row, order_row = facts_t[r : r + 1, :], facts_t[top + r : top + r + 1, :]
        count_col = jnp.zeros((length, 1), jnp.int32)
        count_row = jnp.zeros((1, length), jnp.int32)
        for other in range(top):
            first = (facts_t[other : other + 1, :] == ids_col) & (
                facts_t[top + other : top + other + 1, :] < order_col
            )
            count_col += jnp.sum(first.astype(jnp.int32), axis=1, keepdims=True)
            first = (facts[:, other : other + 1] == ids_row) & (
                facts[:, top + other : top + other + 1] < order_row
            )
            count_row += jnp.sum(first.astype(jnp.int32), axis=0, keepdims=True)
        slot_cols.append(slot_of(ids_col, count_col))
        slot_rows.append(slot_of(ids_row, count_row))

    attn_in.spread(1)
    attn_in.cross(0)
    for j in range(1, GROUP):
        expert_in[0].plane_step(j)
    for k in range(2, planes):
        attn_in.spread(k)
        attn_in.cross(k - 1)
        shared_in.pass_on(k - 1)
    attn_in.cross(planes - 1)
    expert_in[1].start_plane()
    shared_in.start_plane()
    shared_in.over_plane(1)
    attn_in.diagonal()

    small = blocks_of(aw, 4 * heads_width, 4 * heads_width + 128)
    small_rows = small.astype(f32).T
    g_one, g_two = small_rows[0:1, :], small_rows[1:2, :]
    for rows in chunks:
        x = x_ref[rows, :].astype(f32)
        rms = lax.rsqrt(jnp.mean(x * x, axis=-1, keepdims=True) + epsilon)
        xa_ref[rows, :] = (x * rms * g_one).astype(bf16)
    wave, other = waves[...], pltpu.roll(waves[...], 64, 1)
    cosine = jnp.where(lanes() < 64, wave, other)
    sine = jnp.where(lanes() < 64, other, wave)
    pairs = heads_width // 128
    for i, ref in enumerate((q_ref, k_ref)):
        part = dot_nn(xa_ref[...], blocks_of(aw, i * heads_width, (i + 1) * heads_width))
        for g in range(pairs):
            columns = slice(128 * g, 128 * (g + 1))
            ref[:, columns] = turn(part[:, columns], cosine, sine).astype(bf16)
    v_ref[...] = dot_nn(xa_ref[...], blocks_of(aw, 2 * heads_width, 3 * heads_width)).astype(bf16)

    scale = HD ** (-0.5)
    for start, stop in attention_blocks(length):
        logs = jnp.zeros((stop - start, 128), f32)
        for g in range(pairs):
            columns = slice(128 * g, 128 * (g + 1))
            queries = q_ref[start:stop, columns]
            keys, values = k_ref[:stop, columns], v_ref[:stop, columns]
            mixed = []
            for i in range(2):
                one = jnp.where(lanes() // HD == i, queries, jnp.zeros_like(queries))
                scores = dot_nt(one, keys) * scale + bias[start:stop, :stop]
                largest = jnp.max(scores, axis=-1, keepdims=True)
                expo = jnp.exp(scores - largest)
                total = jnp.sum(expo, axis=-1, keepdims=True)
                weights = (expo * (1.0 / total)).astype(bf16)
                mixed.append(dot_nn(weights, values))
                logs = jnp.where(lanes() == LOGS + 2 * g + i, largest + jnp.log(total), logs)
            o_ref[start:stop, columns] = jnp.where(lanes() < HD, mixed[0], mixed[1]).astype(bf16)
            tick(1)
        row_facts[start:stop, :] = logs

    for rows in chunks:
        dx_acc[rows, :] = dot_nt(
            o_ref[rows, :], blocks_of(aw, 3 * heads_width, 4 * heads_width)
        )
    swap = send(dx_acc, gx_ref, twin_sems.at[0, 0], twin_sems.at[1, 0], at.twin())
    swap.start()
    tick(4)
    swap.wait_recv()

    is_expert = (lanes() >= PROBS) & (lanes() < PROBS + experts)
    for rows in chunks:
        h = x_ref[rows, :].astype(f32) + (dx_acc[rows, :] + gx_ref[rows, :])
        gx_ref[rows, :] = h
        rms = lax.rsqrt(jnp.mean(h * h, axis=-1, keepdims=True) + epsilon)
        xf = (h * rms * g_two).astype(bf16)
        xf_ref[rows, :] = xf
        logits = jnp.where(is_expert, dot_nn(xf, small), -1e30)
        expo = jnp.exp(logits - jnp.max(logits, axis=-1, keepdims=True))
        probs = expo / jnp.sum(expo, axis=-1, keepdims=True)
        packed = jnp.where(is_expert, probs, row_facts[rows, :])
        for r in range(top):
            chosen = lanes() == facts[rows, r : r + 1] + PROBS
            gate = jnp.sum(jnp.where(chosen, probs, 0.0), axis=-1, keepdims=True)
            slot = slot_cols[r][rows, :]
            gate = jnp.where(slot >= 0, gate, 0.0)
            packed = jnp.where(lanes() == PAIRS + r, gate, packed)
            packed = jnp.where(lanes() == PAIRS + top + r, slot.astype(f32), packed)
        row_facts[rows, :] = packed
    gate_rows = row_facts[...].T[PAIRS : PAIRS + 8, :]

    def outgoing(j):
        return send(
            placed.at[j * half : (j + 1) * half, :],
            tok.at[0, j],
            token_sems.at[0, j],
            token_sems.at[1, j],
            at.near(j),
        )

    for j in range(experts):
        index = lax.broadcasted_iota(jnp.int32, (half, 1), 0) + j * half
        pick = [slot_rows[r] == index for r in range(top)]
        slot_gate = sum(
            jnp.sum(jnp.where(pick[r], gate_rows[r : r + 1, :], 0.0), axis=1, keepdims=True)
            for r in range(top)
        )
        pick = sum(p.astype(f32) for p in pick).astype(bf16)
        if j:
            target = placed.at[j * half : (j + 1) * half, :]
        else:
            target = tok.at[0, 0]
        target[:, :width] = dot_nn(pick, xf_ref[...]).astype(bf16)
        target[:, width:] = (dot_nn(pick, cot_ref[...]) * slot_gate).astype(bf16)
        if j:
            outgoing(j).start()

    tick(4)
    for j in range(1, experts):
        outgoing(j).wait_recv()
    for k in range(2, planes):
        shared_in.over_plane(k)
    across = send(tok.at[0], tok.at[1], twin_sems.at[0, 1], twin_sems.at[1, 1], at.twin())
    across.start()
    for j in range(1, experts):
        outgoing(j).wait_send()

    def shared_branch():
        shared_in.diagonal()
        shared_in.sent()
        for some in chunks:
            x_t[:, some] = xf_ref[some, :].T
            dy_t[:, some] = cot_ref[some, :].T
        y_acc[...] = jnp.zeros(y_acc.shape, f32)
        dx_acc[...] = jnp.zeros(dx_acc.shape, f32)
        for i in range(2):
            start = s_hidden * i
            branch(
                lambda some: xf_ref[some, :],
                lambda some: cot_ref[some, :],
                slice(0, length),
                sw,
                start,
                2 * s_hidden,
                s_hidden,
                act,
                y_acc,
                dx_acc,
            )

            def shared_grads(plane, carry):
                weight_grads(
                    plane, planes, length, x_t, dy_t, act, s_hidden, sw, start, 2 * s_hidden
                )
                return carry

            lax.fori_loop(0, planes, shared_grads, 0)
            tick(2)
        out_ref[...] = y_acc[...].astype(bf16)
        s_dx[...] = dx_acc[...].astype(bf16)
        swaps = [
            send(mine, theirs, twin_sems.at[0, 2 + i], twin_sems.at[1, 2 + i], at.twin())
            for i, (mine, theirs) in enumerate(((out_ref, ffn_theirs), (s_dx, dx_theirs)))
        ]
        for swap in swaps:
            swap.start()
        return swaps

    across.wait_recv()
    across.wait_send()
    swap.wait_send()

    def home_copy(j):
        return send(
            tok.at[0, j], home.at[0, j], home_sems.at[0, j], home_sems.at[1, j], at.near(j)
        )

    def share(j):
        return send(
            tok.at[1, j],
            ret.at[j * half : (j + 1) * half],
            share_sems.at[0, j],
            share_sems.at[1, j],
            at.twin(),
        )

    for i in range(2):
        expert_in[i].ready()
        expert_in[i].own_sent()

    def expert_half(i):
        for t in (1, 0):
            rows = slice(t * count, (t + 1) * count)

            def x_of(some):
                some = slice(some.start // half, some.stop // half)
                return tok[t, some, :, :width].reshape(-1, width)

            def dy_of(some):
                some = slice(some.start // half, some.stop // half)
                return tok[t, some, :, width:].reshape(-1, width)

            for some in chunks:
                x_t[:, rows.start + some.start : rows.start + some.stop] = x_of(some).T
                dy_t[:, rows.start + some.start : rows.start + some.stop] = dy_of(some).T
            if i == 0:
                y_acc[...] = jnp.zeros(y_acc.shape, f32)
                dx_acc[...] = jnp.zeros(dx_acc.shape, f32)
            else:
                for j in range(experts):
                    some = slice(j * half, (j + 1) * half)
                    y_acc[some, :] = part_one[t, j, :, :width].astype(f32)
                    dx_acc[some, :] = part_one[t, j, :, width:].astype(f32)
            branch(x_of, dy_of, rows, ew.at[i], 0, hidden, hidden, act, y_acc, dx_acc)
            target = tok if i else part_one
            if i and t == 0:
                for j in range(experts):
                    share(j).wait_recv()
            for j in range(experts):
                some = slice(j * half, (j + 1) * half)
                y, dx = y_acc[some, :], dx_acc[some, :]
                if i and t == 0:
                    y += ret[some, :width].astype(f32)
                    dx += ret[some, width:].astype(f32)
                target[t, j, :, :width] = y.astype(bf16)
                target[t, j, :, width:] = dx.astype(bf16)
                if i and t == 0 and j:
                    home_copy(j).start()
            if i and t:
                for j in range(experts):
                    share(j).start()
            tick(2 if i else 2)
        if i:
            home[0, 0] = tok[0, 0]
        expert_in[i].rest_sent()

        def grads_of(n, carry):
            plane = jnp.where(at.z * 2 < planes, planes - 1 - n, n)
            weight_grads(plane, planes, 2 * count, x_t, dy_t, act, hidden, ew.at[i], 0, hidden)
            expert_out[i].start_plane(plane)
            return carry

        lax.fori_loop(0, planes, grads_of, 0)

    while any(getattr(f, "func", None) == expert_in[0].line_step for f in todo):
        tick()
    expert_half(0)
    for k in range(planes):
        shared_in.cross(k)
    swaps = shared_branch()
    tick(len(todo))
    shared_out.start(planes - 1)
    shared_out.start(planes - 2)
    for k in range(planes - 2, 0, -1):
        for j in range(GROUP):
            todo.append(functools.partial(expert_out[0].step, k, j))
        todo.append(functools.partial(shared_out.middle, k + 1))
    expert_half(1)

    for k in range(planes - 3, -1, -1):
        todo.append(functools.partial(shared_out.start, k))
    for k in range(planes - 2, 0, -1):
        for j in range(GROUP):
            todo.append(functools.partial(expert_out[1].step, k, j))
            if k == planes - 2:
                todo.append(functools.partial(expert_out[0].total, j))
    for k in range(planes - 3, -1, -1):
        todo.append(functools.partial(shared_out.middle, k))
    for k in range(planes - 1, 0, -1):
        todo.append(functools.partial(shared_out.step, k))
    for j in range(GROUP):
        todo.append(functools.partial(expert_out[1].total, j))
    for j in range(1, experts):
        home_copy(j).wait_recv()
    swap = send(home.at[0], home.at[1], twin_sems.at[0, 5], twin_sems.at[1, 5], at.twin())
    swap.start()
    tick(2)
    for other in swaps:
        other.wait_recv()
        other.wait_send()
    swap.wait_recv()
    for rows in chunks:
        y = out_ref[rows, :].astype(f32) + ffn_theirs[rows, :].astype(f32)
        dx = s_dx[rows, :].astype(f32) + dx_theirs[rows, :].astype(f32)
        gate = jnp.zeros((step, 128), f32)
        dy = cot_ref[rows, :].astype(f32)
        for core in range(2):
            t = core + at.c - 2 * core * at.c
            index = lax.broadcasted_iota(jnp.int32, (1, count), 1) + t * count
            slots = [row_facts[rows, PAIRS + top + r : PAIRS + top + r + 1] for r in range(top)]
            slots = [(slot.astype(jnp.int32) == index).astype(f32) for slot in slots]
            for r in range(top):
                part = dot_nn(slots[r].astype(bf16), home[t, :, :, :width].reshape(count, width))
                y += row_facts[rows, PAIRS + r : PAIRS + r + 1] * part
                grad = jnp.sum(dy * part, axis=-1, keepdims=True)
                gate += jnp.where(lanes() == facts[rows, r : r + 1] + PROBS, grad, 0.0)
            dx += dot_nn(sum(slots).astype(bf16), home[t, :, :, width:].reshape(count, width))
        out_ref[rows, :] = (gx_ref[rows, :] + y).astype(bf16)
        dx_acc[rows, :] = dx
        y_acc[rows, :128] = gate
    attn_in.sent()

    grad_g_two = jnp.zeros((1, width), f32)
    grad_small = jnp.zeros((width, 128), f32)
    for rows in chunks:
        probs = jnp.where(is_expert, row_facts[rows, :], 0.0)
        grad_probs = y_acc[rows, :128]
        grad_logits = (
            probs * (grad_probs - jnp.sum(probs * grad_probs, axis=-1, keepdims=True))
        ).astype(bf16)
        grad_small += dot_tn(xf_ref[rows, :], grad_logits)
        grad_xf = dx_acc[rows, :] + dot_nt(grad_logits, small)
        h = gx_ref[rows, :]
        grad_h, grad_gain = norm_back_rows(grad_xf, h, g_two)
        grad_g_two += grad_gain
        grad_h = cot_ref[rows, :].astype(f32) + grad_h
        gx_ref[rows, :] = grad_h
        dy_t[:, rows] = grad_h.astype(bf16).T
        grad_o[rows, :] = dot_nn(
            grad_h.astype(bf16), blocks_of(aw, 3 * heads_width, 4 * heads_width)
        ).astype(bf16)
    for rows in chunks:
        x = x_ref[rows, :].astype(f32)
        rms = lax.rsqrt(jnp.mean(x * x, axis=-1, keepdims=True) + epsilon)
        x_t[:, rows] = (x * rms * g_one).astype(bf16).T
    masks()
    tick(2)

    def to_grads(start, columns, left, right):
        blocks = aw.shape[0]
        for i in range(0, blocks, blocks // 4):
            some = slice(i, i + blocks // 4)
            features = slice(i * aw.shape[1], (i + blocks // 4) * aw.shape[1])
            block = dot_nn(left[features, :length], right())
            aw[some, :, start : start + columns] = block.astype(bf16).reshape(
                blocks // 4, aw.shape[1], columns
            )

    to_grads(3 * heads_width, heads_width, dy_t, lambda: o_ref[...])
    for g in range(pairs):
        columns = slice(128 * g, 128 * (g + 1))
        for start, stop in attention_blocks(length)[::-1]:
            queries = q_ref[start:stop, columns]
            grads = grad_o[start:stop, columns]
            keys, values = k_ref[:stop, columns], v_ref[:stop, columns]
            grad_q = jnp.zeros((stop - start, 128), f32)
            grad_k = jnp.zeros((stop, 128), f32)
            grad_v = jnp.zeros((stop, 128), f32)
            for i in range(2):
                mask = lanes() // HD == i
                one_q = jnp.where(mask, queries, jnp.zeros_like(queries))
                one_do = jnp.where(mask, grads, jnp.zeros_like(grads))
                one_k = jnp.where(mask, keys, jnp.zeros_like(keys))
                scores = dot_nt(one_q, keys) * scale + bias[start:stop, :stop]
                log = LOGS + 2 * g + i
                weights = jnp.exp(scores - row_facts[start:stop, log : log + 1])
                grad_w = dot_nt(one_do, values)
                inner = jnp.sum(weights * grad_w, axis=-1, keepdims=True)
                grad_s = (weights * (grad_w - inner)).astype(bf16)
                grad_q += dot_nn(grad_s, one_k)
                grad_k += dot_tn(grad_s, one_q)
                grad_v += dot_tn(weights.astype(bf16), one_do)
            dproj[start:stop, columns] = turn(
                grad_q * scale, cosine[start:stop, :], -sine[start:stop, :]
            ).astype(bf16)
            if stop == length:
                dk_acc[...] = grad_k * scale
                dv_acc[...] = grad_v
            else:
                dk_acc[:stop, :] += grad_k * scale
                dv_acc[:stop, :] += grad_v
            tick(2)
        dproj[:, heads_width + 128 * g : heads_width + 128 * (g + 1)] = turn(
            dk_acc[...], cosine, -sine
        ).astype(bf16)
        dproj[:, 2 * heads_width + 128 * g : 2 * heads_width + 128 * (g + 1)] = dv_acc[
            ...
        ].astype(bf16)
    for rows in chunks:
        part = dot_nt(dproj[rows, :], blocks_of(aw, 0, 3 * heads_width))
        part_mine[rows, :] = part.astype(bf16)
    last_swap = send(part_mine, part_theirs, twin_sems.at[0, 6], twin_sems.at[1, 6], at.twin())
    last_swap.start()
    for i in range(3):
        columns = slice(i * heads_width, (i + 1) * heads_width)
        to_grads(i * heads_width, heads_width, x_t, lambda: dproj[:, columns])
    last_swap.wait_recv()
    grad_g_one = jnp.zeros((1, width), f32)
    for rows in chunks:
        grad_xa = part_mine[rows, :].astype(f32) + part_theirs[rows, :].astype(f32)
        grad_x, grad_gain = norm_back_rows(grad_xa, x_ref[rows, :].astype(f32), g_one)
        gx_ref[rows, :] += grad_x
        grad_g_one += grad_gain
    index = lax.broadcasted_iota(jnp.int32, (128, 1), 0)
    gains = jnp.where(index == 0, grad_g_one, 0.0) + jnp.where(index == 1, grad_g_two, 0.0)
    small_grads = (gains.T + grad_small).astype(bf16)
    aw[:, :, 4 * heads_width :] = small_grads.reshape(aw.shape[0], aw.shape[1], 128)
    for k in range(planes - 1, -1, -1):
        attn_out.start(k)
    tick(3)
    for k in range(planes - 1, -1, -1):
        attn_out.middle(k)
        tick()
    for k in range(planes - 1, 0, -1):
        attn_out.step(k)
        tick()
    tick(len(todo))
    shared_out.total(s_out)
    attn_out.total(a_out)
    for i in range(2):
        for j in range(1, GROUP):
            expert_out[i].arrive(j)

    swap.wait_send()
    last_swap.wait_send()
    for j in range(experts):
        share(j).wait_send()
    for j in range(1, experts):
        home_copy(j).wait_send()
    for i in range(2):
        expert_out[i].sent()
    shared_out.sent()
    attn_out.sent()


def layer(planes, experts, top, heads_width, inputs, own):
    bf16, f32, dma = jnp.bfloat16, jnp.float32, pltpu.SemaphoreType.DMA
    n = planes * GROUP
    length, width = inputs[0].shape
    rows, a_width = own[0].shape
    s_width, e_width = own[1].shape[1], own[2].shape[2] // 2
    half = length * top // experts // 2
    slots = 2 * experts * half
    vmem, anywhere = pl.BlockSpec(memory_space=pltpu.VMEM), pl.BlockSpec(memory_space=pl.ANY)
    shape = jax.ShapeDtypeStruct
    tokens = pltpu.VMEM((2, experts, half, 2 * width), bf16)
    features = pltpu.VMEM((width, slots), bf16)
    wide = pltpu.VMEM((length, width), f32)
    narrow = pltpu.VMEM((length, width), bf16)
    heads = pltpu.VMEM((length, heads_width), bf16)
    facts = pltpu.VMEM((length, 128), f32)

    def plane_buffers(columns):
        return [
            pltpu.VMEM((planes, 2, rows, columns), bf16),
            pltpu.VMEM((planes, rows, columns), bf16),
            pltpu.VMEM((planes + 1, rows, columns), bf16),
        ]

    plane_sems = [dma((2, planes, 2)), dma((2, planes)), dma((2, 2, planes))]
    return pl.pallas_call(
        functools.partial(layer_kernel, planes, experts, top, heads_width),
        out_shape=(
            shape((length, width), bf16),
            shape((length, width), f32),
            shape((rows, a_width), f32),
            shape((rows, s_width), bf16),
            shape((GROUP, rows, 2 * e_width), bf16),
        ),
        in_specs=[vmem] * len(inputs) + [anywhere] * 3,
        out_specs=(vmem,) * 5,
        scratch_shapes=[
            pltpu.VMEM((n, rows, a_width), bf16),
            pltpu.VMEM((n, rows, s_width), bf16),
            pltpu.VMEM((2, n, rows, e_width), bf16),
            tokens,
            tokens,
            tokens,
            pltpu.VMEM((slots, e_width), bf16),
            features,
            features,
            wide,
            wide,
            narrow,
            heads,
            heads,
            heads,
            heads,
            narrow,
            facts,
            narrow,
            narrow,
            pltpu.VMEM((experts * half, 2 * width), bf16),
            *plane_buffers(a_width),
            *plane_buffers(s_width),
            pltpu.VMEM((2, (planes + 1) * GROUP, rows, e_width), bf16),
            dma((10,)),
            dma((n,)),
            dma((4, n)),
            dma((n,)),
            dma((4, n)),
            dma((2, n)),
            dma((2, 2, n)),
            dma((2, GROUP)),
            *plane_sems,
            *plane_sems,
            dma((2, 2, 2, n)),
            dma((2, 2, GROUP, 3)),
            dma((2, GROUP)),
            dma((2, GROUP)),
            dma((2, GROUP)),
            dma((2, 7)),
        ],
        compiler_params=pltpu.CompilerParams(
            collective_id=0, has_side_effects=True, vmem_limit_bytes=63 << 20
        ),
    )(*inputs, *own)


def local_grouped(
    planes,
    tokens,
    segment_ids,
    expert_ids,
    slot_order,
    gain_attn,
    qkv_weight,
    out_weight,
    gain_ffn,
    router_weight,
    gate_up,
    down_weight,
    shared_gate_up,
    shared_down,
    cotangent,
):
    bf16, f32 = jnp.bfloat16, jnp.float32
    rows, heads_width = qkv_weight.shape[0], qkv_weight.shape[2]
    experts, hidden = down_weight.shape[0], down_weight.shape[1]
    s_hidden = shared_down.shape[0]
    length = tokens.shape[0]
    top = expert_ids.shape[1]
    cuts = [3 * heads_width, heads_width, 128]
    edges = [sum(cuts[:i]) for i in range(len(cuts) + 1)]

    def part(array, i):
        return array[..., edges[i] : edges[i + 1]]

    expert_packed = jnp.concatenate(
        [gate_up.reshape(experts, rows, 2 * hidden), down_weight.transpose(0, 2, 1)], axis=2
    )
    shared_packed = jnp.concatenate(
        [shared_gate_up.reshape(rows, 2 * s_hidden), shared_down.T], axis=1
    )
    small = jnp.concatenate([gain_attn[:, None], gain_ffn[:, None], router_weight], axis=1)
    small = jnp.pad(small, ((0, 0), (0, 128 - small.shape[1])))
    attn_packed = jnp.concatenate(
        [qkv_weight.reshape(rows, 3 * heads_width), out_weight.T, small], axis=1
    )
    cosine, sine = rotary(length, HD)
    waves = jnp.concatenate([cosine[:, 0]] * 2 + [sine[:, 0]] * 2, axis=1)
    facts = jnp.concatenate(
        [expert_ids, slot_order.reshape(length, top), segment_ids.reshape(length, 1)], axis=1
    )
    facts = jnp.pad(facts, ((0, 0), (0, 8 - facts.shape[1])))
    output, grad_tokens, mine, mine_shared, mine_expert = layer(
        planes,
        experts,
        top,
        heads_width,
        (tokens, cotangent, facts, facts.T, waves),
        (attn_packed, shared_packed, expert_packed),
    )
    small_mine = part(mine, 2)
    mine_shared, mine_expert = mine_shared.astype(f32), mine_expert.astype(f32)
    return (
        output,
        grad_tokens,
        small_mine[:, 0],
        part(mine, 0).reshape(rows, 3, heads_width),
        part(mine, 1).T,
        small_mine[:, 1],
        small_mine[:, 2 : 2 + experts],
        mine_expert[:, :, : 2 * hidden].reshape(experts, rows, 2, hidden),
        mine_expert[:, :, 2 * hidden :].transpose(0, 2, 1),
        mine_shared[:, : 2 * s_hidden].reshape(rows, 2, s_hidden),
        mine_shared[:, 2 * s_hidden :].T,
    )


def solution(mesh):
    def pick(*args):
        experts, rows = args[9].shape[0], args[5].shape[0]
        if experts == GROUP and mesh.shape["dp"] % GROUP == 0 and rows % 16 == 0:
            return local_grouped(mesh.shape["dp"] // GROUP, *args)
        return local_plain(*args)

    return jax.shard_map(
        pick,
        mesh=mesh,
        in_specs=(
            P("dp", None),
            P("dp", None),
            P("dp", None),
            P("dp", None),
            P("dp"),
            P("dp", None, "tensor"),
            P("tensor", "dp"),
            P("dp"),
            P("dp", None),
            P(None, "dp", None, "tensor"),
            P(None, "tensor", "dp"),
            P("dp", None, "tensor"),
            P("tensor", "dp"),
            P("dp", None),
        ),
        out_specs=(
            P("dp", None),
            P("dp", None),
            P("dp"),
            P("dp", None, "tensor"),
            P("tensor", "dp"),
            P("dp"),
            P("dp", None),
            P(None, "dp", None, "tensor"),
            P(None, "tensor", "dp"),
            P("dp", None, "tensor"),
            P("tensor", "dp"),
        ),
        check_vma=False,
    )
```

profile of v0, /device:TPU:8, one launch (start us, length us, event | category | flops | bytes accessed | tf_op | source)
XLA Modules:
  0.0 270.2 jit_solution(2654336217800191364)
XLA Ops:
  0.6 0.0 copy-start.11
  0.7 0.0 copy-start.10
  0.7 0.0 copy-start.3
  0.7 1.0 multiply_cosine_fusion
  1.7 1.0 pad_maximum_fusion.2.waves
  2.7 0.0 copy-start.5
  2.7 0.5 broadcast.17
  3.2 1.3 reduce.7
  4.5 0.2 reshape.56
  4.7 0.1 copy.46
  4.8 0.0 copy-done.11
  4.8 0.0 copy-done.10
  4.9 0.1 copy.57
  5.0 0.7 pad.8.clone.facts
  5.8 0.6 pad_bitcast_fusion.facts_t
  6.4 0.0 copy-done.3
  6.4 0.6 reshape.60
  7.0 0.0 copy-start.6
  7.0 0.0 copy-start.8
  7.0 0.0 copy-done.5
  7.0 0.0 copy-start.7
  7.0 0.0 copy-start.12
  7.0 0.0 copy-start.13
  7.0 0.0 copy-start.14
  7.0 0.0 copy-start.9
  7.1 1.1 pad_maximum_fusion.e_own
  8.2 0.0 copy-done.6
  8.2 0.0 copy-done.8
  8.2 0.7 pad_maximum_fusion.1.s_own
  9.0 0.0 copy-done.7
  9.0 0.0 copy-done.12
  9.0 0.0 copy-done.13
  9.0 0.0 copy-done.14
  9.0 0.1 copy.49
  9.1 0.0 copy-done.9
  9.1 0.7 fusion.1.a_own
  9.8 245.1 %shard_map.221 = (bf16[512,768]{1,0:T(8,128)(2,1)}, f32[512,768]{1,0:T(8,128)}, f32[48,1664]{1,0:T(8,128)}, bf16[48,3072]{1,0:T(8,128)(2,1)}, bf16[4,48,3072]{2,1,0:T(8,128)(2,1)}) custom-call(bf16[512,768]{1,0:T(8,128)(2,1)} %x_ref.1, bf16[512,768]{1,0:T(8,128)(2,1)} %cot_ref.1, s32[512,8]{1,0:T(8,128)} %pad.8.clone.facts, ...), custom_call_target="tpu_custom_call" | custom-call | tf_op jit(solution)/shard_map/pallas_call | solution.py:1602
  254.9 1.5 slice_reduce_fusion
  256.4 0.9 slice.32
  257.4 0.7 copy.58
  258.1 1.5 slice_bitcast_fusion.2
  259.6 0.8 slice.35
  260.4 0.7 copy.52
  261.1 1.3 slice.40
  262.4 0.0 copy-start
  262.4 2.5 reshape.62
  264.9 0.0 copy-done
  264.9 0.3 convert_element_type.36
  265.1 0.0 copy-start.1
  265.1 1.0 slice_bitcast_fusion
  266.1 0.0 copy-start.4
  266.1 0.0 copy-done.1
  266.1 1.1 reshape.63
  267.2 0.0 copy-start.2
  267.2 0.7 slice_bitcast_fusion.1
  267.9 0.0 copy-done.4
  267.9 0.9 copy.61
  268.8 0.0 copy-done.2
  268.8 1.1 copy.62
  (8 shorter events, 0.2 us)
Async XLA Ops:
  0.6 4.2 %copy-start.11 = (s32[1,512]{1,0:T(1,128)S(1)}, s32[1,512]{1,0:T(1,128)}, u32[]{:S(2)}) copy-start(s32[1,512]{1,0:T(1,128)} %param.15) | copy-start | bytes 6148
  0.7 4.2 %copy-start.10 = (s32[512,2]{0,1:T(2,128)S(1)}, s32[512,2]{0,1:T(2,128)}, u32[]{:S(2)}) copy-start(s32[512,2]{0,1:T(2,128)} %param.16) | copy-start | bytes 12292
  0.7 5.7 %copy-start.3 = (bf16[4,48,2,1024]{3,2,1,0:T(2,128)(2,1)S(1)}, bf16[4,48,2,1024]{3,2,1,0:T(2,128)(2,1)}, u32[]{:S(2)}) copy-start(bf16[4,48,2,1024]{3,2,1,0:T(2,128)(2,1)} %param.23) | copy-start | bytes 2359300
  2.7 4.3 %copy-start.5 = (bf16[4,1024,48]{1,2,0:T(8,128)(2,1)S(1)}, bf16[4,1024,48]{1,2,0:T(8,128)(2,1)}, u32[]{:S(2)}) copy-start(bf16[4,1024,48]{1,2,0:T(8,128)(2,1)} %param.24) | copy-start | bytes 1179652
  7.0 1.2 copy-start.6
  7.0 1.2 copy-start.8
  7.0 2.0 copy-start.7
  7.0 2.0 copy-start.12
  7.0 2.0 copy-start.13
  7.0 2.0 copy-start.14
  7.0 2.1 copy-start.9
  262.4 2.5 copy-start
  265.1 1.0 copy-start.1
  266.1 1.8 copy-start.4
  267.2 1.6 copy-start.2
where the time goes:
time: 274 us; the launch traced here: 270 us
  Pallas kernels  245 us (89%)
  local copies, waits for them, and re-layouts  17.8 us (6%)
  other arithmetic  6.17 us (2%)
    pallas_call x1, Pallas kernels, layer(): pl.pallas_call(functools.partial(layer_kernel, planes, experts, top, head...  245 us

commit v1 on v0

--- a/solution.py
+++ b/solution.py
@@ -963,6 +963,174 @@
 
 
 PROBS, PAIRS, LOGS = 2, 8, 16
+
+
+PLAN = {
+    "begin": [
+        ("E own", 0),
+        ("S own",),
+    ],
+    "gather 1": [
+        ("S plane",),
+    ],
+    "gather 2": [
+        ("S line", 1),
+        ("E line", 0, 1, 0),
+    ],
+    "gather 3": [
+        ("E across", 1),
+        ("E plane", 0, 1),
+        ("S line", 2),
+        ("E plane", 0, 2),
+        ("E plane", 0, 3),
+    ],
+    "gathered": [
+        ("S over", 2),
+        ("E line", 0, 2, 0),
+        ("S line", 3),
+        ("S over", 1),
+        ("S over", 3),
+        ("E own", 1),
+    ],
+    "projected": [],
+    "attention 0 0": [
+        ("E line", 0, 1, 2),
+    ],
+    "attention 0 1": [],
+    "attention 0 2": [
+        ("E line", 0, 1, 3),
+    ],
+    "attention 1 0": [
+        ("S cross", 2),
+    ],
+    "attention 1 1": [
+        ("S cross", 1),
+    ],
+    "attention 1 2": [
+        ("E line", 0, 1, 1),
+    ],
+    "attended": [
+        ("E line", 0, 2, 2),
+        ("E plane", 1, 1),
+        ("E plane", 1, 2),
+        ("E plane", 1, 3),
+        ("E line", 1, 1, 0),
+        ("S cross", 3),
+        ("S cross", 0),
+    ],
+    "dispatched": [
+        ("E line", 0, 2, 3),
+        ("E line", 0, 3, 2),
+    ],
+    "shared 0": [
+        ("E line", 0, 2, 1),
+        ("E line", 1, 1, 2),
+        ("E line", 1, 1, 3),
+        ("E line", 1, 1, 1),
+        ("E line", 0, 3, 0),
+    ],
+    "shared 1": [],
+    "shared": [
+        ("S start", 2),
+        ("S start", 1),
+    ],
+    "arrived": [
+        ("E line", 0, 3, 1),
+        ("E line", 0, 3, 3),
+        ("E line", 1, 2, 0),
+        ("E line", 1, 2, 1),
+        ("E line", 1, 2, 2),
+        ("E line", 1, 2, 3),
+        ("S start", 3),
+    ],
+    "expert 0 1": [],
+    "expert 0 0": [],
+    "expert 0": [
+        ("E line", 1, 3, 0),
+        ("E line", 1, 3, 1),
+        ("E line", 1, 3, 2),
+        ("E line", 1, 3, 3),
+    ],
+    "expert 1 1": [
+        ("E step", 0, 2, 0),
+    ],
+    "expert 1 0": [
+        ("E step", 0, 2, 3),
+        ("S start", 0),
+    ],
+    "expert 1": [
+        ("E step", 0, 2, 2),
+        ("E step", 0, 2, 1),
+        ("E step", 0, 1, 0),
+        ("E step", 0, 1, 2),
+        ("E step", 0, 1, 3),
+    ],
+    "home": [
+        ("E step", 0, 1, 1),
+        ("S middle", 3),
+        ("S middle", 0),
+    ],
+    "combined": [],
+    "projected out": [
+        ("A start", 0, 3),
+        ("A start", 0, 2),
+        ("A start", 0, 1),
+        ("A start", 0, 0),
+    ],
+    "backward 0 1": [
+        ("E total", 0, 1),
+        ("E total", 0, 2),
+        ("E total", 0, 3),
+        ("S middle", 1),
+        ("E total", 0, 0),
+    ],
+    "backward 0 0": [
+        ("E step", 1, 2, 0),
+        ("E step", 1, 2, 1),
+        ("E step", 1, 2, 3),
+        ("S step", 3),
+    ],
+    "backward 1 1": [],
+    "backward 1 0": [
+        ("E step", 1, 1, 0),
+    ],
+    "backward 2 1": [],
+    "backward 2 0": [
+        ("S middle", 2),
+    ],
+    "projected back": [
+        ("E step", 1, 2, 2),
+        ("E step", 1, 1, 2),
+        ("E step", 1, 1, 1),
+    ],
+    "last": [
+        ("A start", 1, 3),
+        ("A start", 1, 0),
+        ("A start", 1, 1),
+        ("E step", 1, 1, 3),
+        ("A middle", 0, 3),
+        ("A middle", 1, 3),
+        ("A start", 1, 2),
+        ("A middle", 0, 2),
+        ("A middle", 1, 2),
+        ("A step", 0, 3),
+        ("A step", 1, 3),
+        ("A middle", 0, 1),
+        ("A middle", 1, 1),
+        ("S step", 2),
+        ("E total", 1, 0),
+        ("E total", 1, 1),
+        ("E total", 1, 2),
+        ("E total", 1, 3),
+        ("A step", 0, 2),
+        ("A step", 1, 2),
+        ("A middle", 0, 0),
+        ("A middle", 1, 0),
+        ("S step", 1),
+        ("A step", 0, 1),
+        ("A step", 1, 1),
+    ],
+}
 
 
 def layer_kernel(
@@ -1068,10 +1236,22 @@
         for i in range(2)
     ]
     shared_out = PlaneSum(at, sw, s_one, s_two, s_came, s_one_sems, s_two_sems, s_line_sems)
-    attn_out = PlaneSum(at, aw, a_one, a_two, a_came, a_one_sems, a_two_sems, a_line_sems)
+    attn_out = [
+        PlaneSum(
+            at,
+            aw.at[:, :, columns],
+            a_one.at[:, :, :, columns],
+            a_two.at[:, :, columns],
+            a_came.at[:, :, columns],
+            a_one_sems.at[i],
+            a_two_sems.at[i],
+            a_line_sems.at[i],
+        )
+        for i, columns in enumerate((slice(0, heads_width), slice(heads_width, aw.shape[2])))
+    ]
 
     xa_ref = act.at[:length, :width]
-    placed = act.at[:, : 2 * width]
+    placed = ret
     part_mine = act.at[length:, :width]
     part_theirs = ret.at[:length, :width]
     grad_o = act.at[:length, :heads_width]
@@ -1095,32 +1275,38 @@
     for k in range(3):
         halve(0, k).wait()
     expert_in[0].start_plane()
-    expert_in[0].start_line()
-    shared_in.start_line()
     for k in range(3):
         halve(1, k).wait()
 
-    todo = []
-
-    def tick(amount=1):
-        for _ in range(amount):
-            if todo:
-                todo.pop(0)()
-
-    def lines(i, k, members=range(GROUP)):
-        return [functools.partial(expert_in[i].line_step, k, j) for j in members]
-
-    def second_half():
-        expert_in[1].start_line()
-        for j in range(1, GROUP):
-            expert_in[1].plane_step(j)
-
-    todo += lines(0, 1)
-    todo.append(second_half)
-    todo.append(functools.partial(shared_in.pass_on, planes - 1))
-    for k in range(2, planes):
-        todo += lines(0, k) + lines(1, k - 1)
-    todo += lines(1, planes - 1)
+    def turn_of(name):
+        for step in PLAN[name]:
+            do(*step)
+
+    def do(kind, *numbers):
+        steps[kind](*numbers)
+
+    steps = {
+        "E plane": lambda i, j: expert_in[i].plane_step(j),
+        "E across": lambda i: expert_in[i].start_plane(),
+        "E own": lambda i: expert_in[i].start_line(),
+        "E line": lambda i, k, j: expert_in[i].line_step(k, j),
+        "S own": lambda: shared_in.start_line(),
+        "S plane": lambda: shared_in.start_plane(),
+        "S line": lambda k: shared_in.pass_on(k),
+        "S over": lambda k: shared_in.over_plane(k),
+        "S cross": lambda k: shared_in.cross(k),
+        "S start": lambda k: shared_out.start(k),
+        "S middle": lambda k: shared_out.middle(k),
+        "S step": lambda k: shared_out.step(k),
+        "E step": lambda i, k, j: expert_out[i].step(k, j),
+        "E total": lambda i, j: expert_out[i].total(j),
+        "A start": lambda i, k: attn_out[i].start(k),
+        "A middle": lambda i, k: attn_out[i].middle(k),
+        "A step": lambda i, k: attn_out[i].step(k),
+    }
+
+    turn_of("begin")
+
     def masks():
         for start, stop in attention_blocks(length):
             row = lax.broadcasted_iota(jnp.int32, (stop - start, stop), 0) + start
@@ -1157,18 +1343,12 @@
         slot_cols.append(slot_of(ids_col, count_col))
         slot_rows.append(slot_of(ids_row, count_row))
 
-    attn_in.spread(1)
-    attn_in.cross(0)
-    for j in range(1, GROUP):
-        expert_in[0].plane_step(j)
-    for k in range(2, planes):
+    for k in range(1, planes):
         attn_in.spread(k)
         attn_in.cross(k - 1)
-        shared_in.pass_on(k - 1)
+        turn_of(f"gather {k}")
     attn_in.cross(planes - 1)
-    expert_in[1].start_plane()
-    shared_in.start_plane()
-    shared_in.over_plane(1)
+    turn_of("gathered")
     attn_in.diagonal()
 
     small = blocks_of(aw, 4 * heads_width, 4 * heads_width + 128)
@@ -1183,11 +1363,12 @@
     sine = jnp.where(lanes() < 64, other, wave)
     pairs = heads_width // 128
     for i, ref in enumerate((q_ref, k_ref)):
-        part = dot_nn(xa_ref[...], blocks_of(aw, i * heads_width, (i + 1) * heads_width))
+        part = dot_nn(xa_ref[...], blocks_of(aw, (i + 1) * heads_width, (i + 2) * heads_width))
         for g in range(pairs):
             columns = slice(128 * g, 128 * (g + 1))
             ref[:, columns] = turn(part[:, columns], cosine, sine).astype(bf16)
-    v_ref[...] = dot_nn(xa_ref[...], blocks_of(aw, 2 * heads_width, 3 * heads_width)).astype(bf16)
+    v_ref[...] = dot_nn(xa_ref[...], blocks_of(aw, 3 * heads_width, 4 * heads_width)).astype(bf16)
+    turn_of("projected")
 
     scale = HD ** (-0.5)
     for start, stop in attention_blocks(length):
@@ -1207,16 +1388,16 @@
                 mixed.append(dot_nn(weights, values))
                 logs = jnp.where(lanes() == LOGS + 2 * g + i, largest + jnp.log(total), logs)
             o_ref[start:stop, columns] = jnp.where(lanes() < HD, mixed[0], mixed[1]).astype(bf16)
-            tick(1)
+            turn_of(f"attention {start // (length // 2)} {g}")
         row_facts[start:stop, :] = logs
 
     for rows in chunks:
         dx_acc[rows, :] = dot_nt(
-            o_ref[rows, :], blocks_of(aw, 3 * heads_width, 4 * heads_width)
+            o_ref[rows, :], blocks_of(aw, 0, heads_width)
         )
     swap = send(dx_acc, gx_ref, twin_sems.at[0, 0], twin_sems.at[1, 0], at.twin())
     swap.start()
-    tick(4)
+    turn_of("attended")
     swap.wait_recv()
 
     is_expert = (lanes() >= PROBS) & (lanes() < PROBS + experts)
@@ -1265,16 +1446,6 @@
         target[:, width:] = (dot_nn(pick, cot_ref[...]) * slot_gate).astype(bf16)
         if j:
             outgoing(j).start()
-
-    tick(4)
-    for j in range(1, experts):
-        outgoing(j).wait_recv()
-    for k in range(2, planes):
-        shared_in.over_plane(k)
-    across = send(tok.at[0], tok.at[1], twin_sems.at[0, 1], twin_sems.at[1, 1], at.twin())
-    across.start()
-    for j in range(1, experts):
-        outgoing(j).wait_send()
 
     def shared_branch():
         shared_in.diagonal()
@@ -1306,7 +1477,7 @@
                 return carry
 
             lax.fori_loop(0, planes, shared_grads, 0)
-            tick(2)
+            turn_of(f"shared {i}")
         out_ref[...] = y_acc[...].astype(bf16)
         s_dx[...] = dx_acc[...].astype(bf16)
         swaps = [
@@ -1317,9 +1488,19 @@
             swap.start()
         return swaps
 
+    turn_of("dispatched")
+    swap.wait_send()
+    swaps = shared_branch()
+    turn_of("shared")
+    for j in range(1, experts):
+        outgoing(j).wait_recv()
+        outgoing(j).wait_send()
+    across = send(tok.at[0], tok.at[1], twin_sems.at[0, 1], twin_sems.at[1, 1], at.twin())
+    across.start()
+    turn_of("arrived")
+
     across.wait_recv()
     across.wait_send()
-    swap.wait_send()
 
     def home_copy(j):
         return send(
@@ -1380,7 +1561,7 @@
             if i and t:
                 for j in range(experts):
                     share(j).start()
-            tick(2 if i else 2)
+            turn_of(f"expert {i} {t}")
         if i:
             home[0, 0] = tok[0, 0]
         expert_in[i].rest_sent()
@@ -1393,39 +1574,15 @@
 
         lax.fori_loop(0, planes, grads_of, 0)
 
-    while any(getattr(f, "func", None) == expert_in[0].line_step for f in todo):
-        tick()
-    expert_half(0)
-    for k in range(planes):
-        shared_in.cross(k)
-    swaps = shared_branch()
-    tick(len(todo))
-    shared_out.start(planes - 1)
-    shared_out.start(planes - 2)
-    for k in range(planes - 2, 0, -1):
-        for j in range(GROUP):
-            todo.append(functools.partial(expert_out[0].step, k, j))
-        todo.append(functools.partial(shared_out.middle, k + 1))
-    expert_half(1)
-
-    for k in range(planes - 3, -1, -1):
-        todo.append(functools.partial(shared_out.start, k))
-    for k in range(planes - 2, 0, -1):
-        for j in range(GROUP):
-            todo.append(functools.partial(expert_out[1].step, k, j))
-            if k == planes - 2:
-                todo.append(functools.partial(expert_out[0].total, j))
-    for k in range(planes - 3, -1, -1):
-        todo.append(functools.partial(shared_out.middle, k))
-    for k in range(planes - 1, 0, -1):
-        todo.append(functools.partial(shared_out.step, k))
-    for j in range(GROUP):
-        todo.append(functools.partial(expert_out[1].total, j))
+    for i in range(2):
+        expert_half(i)
+        turn_of(f"expert {i}")
+
     for j in range(1, experts):
         home_copy(j).wait_recv()
     swap = send(home.at[0], home.at[1], twin_sems.at[0, 5], twin_sems.at[1, 5], at.twin())
     swap.start()
-    tick(2)
+    turn_of("home")
     for other in swaps:
         other.wait_recv()
         other.wait_send()
@@ -1468,14 +1625,14 @@
         gx_ref[rows, :] = grad_h
         dy_t[:, rows] = grad_h.astype(bf16).T
         grad_o[rows, :] = dot_nn(
-            grad_h.astype(bf16), blocks_of(aw, 3 * heads_width, 4 * heads_width)
+            grad_h.astype(bf16), blocks_of(aw, 0, heads_width)
         ).astype(bf16)
     for rows in chunks:
         x = x_ref[rows, :].astype(f32)
         rms = lax.rsqrt(jnp.mean(x * x, axis=-1, keepdims=True) + epsilon)
         x_t[:, rows] = (x * rms * g_one).astype(bf16).T
     masks()
-    tick(2)
+    turn_of("combined")
 
     def to_grads(start, columns, left, right):
         blocks = aw.shape[0]
@@ -1487,7 +1644,8 @@
                 blocks // 4, aw.shape[1], columns
             )
 
-    to_grads(3 * heads_width, heads_width, dy_t, lambda: o_ref[...])
+    to_grads(0, heads_width, dy_t, lambda: o_ref[...])
+    turn_of("projected out")
     for g in range(pairs):
         columns = slice(128 * g, 128 * (g + 1))
         for start, stop in attention_blocks(length)[::-1]:
@@ -1520,7 +1678,7 @@
             else:
                 dk_acc[:stop, :] += grad_k * scale
                 dv_acc[:stop, :] += grad_v
-            tick(2)
+            turn_of(f"backward {g} {start // (length // 2)}")
         dproj[:, heads_width + 128 * g : heads_width + 128 * (g + 1)] = turn(
             dk_acc[...], cosine, -sine
         ).astype(bf16)
@@ -1528,13 +1686,14 @@
             ...
         ].astype(bf16)
     for rows in chunks:
-        part = dot_nt(dproj[rows, :], blocks_of(aw, 0, 3 * heads_width))
+        part = dot_nt(dproj[rows, :], blocks_of(aw, heads_width, 4 * heads_width))
         part_mine[rows, :] = part.astype(bf16)
     last_swap = send(part_mine, part_theirs, twin_sems.at[0, 6], twin_sems.at[1, 6], at.twin())
     last_swap.start()
     for i in range(3):
         columns = slice(i * heads_width, (i + 1) * heads_width)
-        to_grads(i * heads_width, heads_width, x_t, lambda: dproj[:, columns])
+        to_grads((i + 1) * heads_width, heads_width, x_t, lambda: dproj[:, columns])
+    turn_of("projected back")
     last_swap.wait_recv()
     grad_g_one = jnp.zeros((1, width), f32)
     for rows in chunks:
@@ -1546,18 +1705,10 @@
     gains = jnp.where(index == 0, grad_g_one, 0.0) + jnp.where(index == 1, grad_g_two, 0.0)
     small_grads = (gains.T + grad_small).astype(bf16)
     aw[:, :, 4 * heads_width :] = small_grads.reshape(aw.shape[0], aw.shape[1], 128)
-    for k in range(planes - 1, -1, -1):
-        attn_out.start(k)
-    tick(3)
-    for k in range(planes - 1, -1, -1):
-        attn_out.middle(k)
-        tick()
-    for k in range(planes - 1, 0, -1):
-        attn_out.step(k)
-        tick()
-    tick(len(todo))
+    turn_of("last")
     shared_out.total(s_out)
-    attn_out.total(a_out)
+    for i, columns in enumerate((slice(0, heads_width), slice(heads_width, aw.shape[2]))):
+        attn_out[i].total(a_out.at[:, columns])
     for i in range(2):
         for j in range(1, GROUP):
             expert_out[i].arrive(j)
@@ -1571,7 +1722,8 @@
     for i in range(2):
         expert_out[i].sent()
     shared_out.sent()
-    attn_out.sent()
+    for i in range(2):
+        attn_out[i].sent()
 
 
 def layer(planes, experts, top, heads_width, inputs, own):
@@ -1643,7 +1795,7 @@
             dma((2, n)),
             dma((2, 2, n)),
             dma((2, GROUP)),
-            *plane_sems,
+            *[dma((2,) + s.shape) for s in plane_sems],
             *plane_sems,
             dma((2, 2, 2, n)),
             dma((2, 2, GROUP, 3)),
@@ -1681,7 +1833,7 @@
     s_hidden = shared_down.shape[0]
     length = tokens.shape[0]
     top = expert_ids.shape[1]
-    cuts = [3 * heads_width, heads_width, 128]
+    cuts = [heads_width, 3 * heads_width, 128]
     edges = [sum(cuts[:i]) for i in range(len(cuts) + 1)]
 
     def part(array, i):
@@ -1696,7 +1848,7 @@
     small = jnp.concatenate([gain_attn[:, None], gain_ffn[:, None], router_weight], axis=1)
     small = jnp.pad(small, ((0, 0), (0, 128 - small.shape[1])))
     attn_packed = jnp.concatenate(
-        [qkv_weight.reshape(rows, 3 * heads_width), out_weight.T, small], axis=1
+        [out_weight.T, qkv_weight.reshape(rows, 3 * heads_width), small], axis=1
     )
     cosine, sine = rotary(length, HD)
     waves = jnp.concatenate([cosine[:, 0]] * 2 + [sine[:, 0]] * 2, axis=1)
@@ -1713,19 +1865,23 @@
         (attn_packed, shared_packed, expert_packed),
     )
     small_mine = part(mine, 2)
-    mine_shared, mine_expert = mine_shared.astype(f32), mine_expert.astype(f32)
+
+    def halves(grads, size):
+        both = [grads[..., :size], grads[..., size : 2 * size]]
+        return jnp.stack(both, axis=-2).astype(f32)
+
     return (
         output,
         grad_tokens,
         small_mine[:, 0],
-        part(mine, 0).reshape(rows, 3, heads_width),
-        part(mine, 1).T,
+        part(mine, 1).reshape(rows, 3, heads_width),
+        part(mine, 0).T,
         small_mine[:, 1],
         small_mine[:, 2 : 2 + experts],
-        mine_expert[:, :, : 2 * hidden].reshape(experts, rows, 2, hidden),
-        mine_expert[:, :, 2 * hidden :].transpose(0, 2, 1),
-        mine_shared[:, : 2 * s_hidden].reshape(rows, 2, s_hidden),
-        mine_shared[:, 2 * s_hidden :].T,
+        halves(mine_expert, hidden),
+        mine_expert[:, :, 2 * hidden :].transpose(0, 2, 1).astype(f32),
+        halves(mine_shared, s_hidden),
+        mine_shared[:, 2 * s_hidden :].T.astype(f32),
     )
 
 

time: 274 us -> 251 us (0.916)
  Pallas kernels: 245 us -> 222 us
  other arithmetic: 6.17 us -> 9.72 us
  local copies, waits for them, and re-layouts: 17.8 us -> 14.7 us
    pallas_call x1, Pallas kernels: 245 us -> 222 us  [layer(): pl.pallas_call(functools.partial(layer_kernel, planes, experts, top, head...]
    reshape x3 -> x1, local copies, waits for them, and re-layouts: 4.25 us -> 0.7 us  [local_grouped(): part(mine, 1).reshape(rows, 3, heads_width)]
    unnamed x36 -> x32, local copies, waits for them, and re-layouts: 3.45 us -> 6.83 us
    convert_element_type x2 -> x4, other arithmetic: 0.29 us -> 3.1 us  [the longest x1 2.26 us: local_grouped(): mine_expert[:, :, 2 * hidden:].transpose(0, 2, 1).astype(f32)]
where the time goes in v1:
time: 251 us; the launch traced here: 248 us
  Pallas kernels  222 us (88%)
  local copies, waits for them, and re-layouts  14.7 us (6%)
  other arithmetic  9.72 us (4%)
    pallas_call x1, Pallas kernels, layer(): pl.pallas_call(functools.partial(layer_kernel, planes, experts, top, head...  222 us
    unnamed x32, local copies, waits for them, and re-layouts  6.83 us

profile of v1, /device:TPU:8, one launch (start us, length us, event | category | flops | bytes accessed | tf_op | source)
XLA Modules:
  0.0 247.5 jit_solution(1573341401268557788)
XLA Ops:
  0.6 0.0 copy-start.9
  0.7 0.0 copy-start.10
  0.7 0.0 copy-start.11
  0.7 0.0 copy-start.6
  0.7 0.0 copy-start.8
  0.7 0.5 broadcast.17
  1.2 1.3 reduce.7
  2.6 0.2 reshape.50
  2.8 0.0 copy-start.5
  2.8 0.1 copy.52
  2.9 0.0 copy-start.7
  2.9 0.8 pad_add_fusion
  3.6 0.1 copy.65
  3.8 0.7 pad.8.clone.facts
  4.5 0.0 copy-start.1
  4.5 0.6 pad_bitcast_fusion.facts_t
  5.2 1.0 multiply_cosine_fusion
  6.1 1.0 pad_maximum_fusion.2.waves
  7.1 0.0 copy-start.3
  7.1 0.0 copy-done.9
  7.1 0.0 copy-done.10
  7.1 0.0 copy-done.11
  7.2 0.1 copy.55
  7.3 0.0 copy-done.6
  7.3 0.0 copy-done.8
  7.3 0.7 fusion.1.a_own
  8.0 0.0 copy-done.5
  8.0 0.0 copy-done.7
  8.0 0.7 pad_maximum_fusion.1.s_own
  8.8 0.0 copy-done.1
  8.8 0.6 reshape.54
  9.4 0.0 copy-done.3
  9.4 1.1 pad_maximum_fusion.e_own
  10.5 222.1 %shard_map.221 = (bf16[512,768]{1,0:T(8,128)(2,1)}, f32[512,768]{1,0:T(8,128)}, f32[48,1664]{1,0:T(8,128)}, bf16[48,3072]{1,0:T(8,128)(2,1)}, bf16[4,48,3072]{2,1,0:T(8,128)(2,1)}) custom-call(bf16[512,768]{1,0:T(8,128)(2,1)} %x_ref.1, bf16[512,768]{1,0:T(8,128)(2,1)} %cot_ref.1, s32[512,8]{1,0:T(8,128)} %pad.8.clone.facts, ...), custom_call_target="tpu_custom_call" | custom-call | tf_op jit(solution)/shard_map/pallas_call | solution.py:1754
  232.6 1.5 slice_reduce_fusion
  234.1 0.9 slice.38
  235.0 0.7 copy.66
  235.8 1.5 slice_bitcast_fusion.4
  237.3 0.8 slice.41
  238.1 0.7 copy.58
  238.7 2.3 convert_bitcast_fusion
  241.0 0.1 maximum_convert_fusion
  241.1 0.0 copy-start.4
  241.1 2.4 copy.59
  243.5 0.0 copy-start.2
  243.5 0.0 copy-done.4
  243.5 0.7 convert_bitcast_fusion.1
  244.2 0.0 copy-start
  244.2 1.1 copy.60
  245.3 0.0 copy-done.2
  245.3 0.9 copy.69
  246.2 0.0 copy-done
  246.2 1.1 copy.70
  (6 shorter events, 0.1 us)
Async XLA Ops:
  0.6 6.5 %copy-start.9 = (bf16[48,4]{0,1:T(4,128)(2,1)S(1)}, bf16[48,4]{0,1:T(4,128)(2,1)}, u32[]{:S(2)}) copy-start(bf16[48,4]{0,1:T(4,128)(2,1)} %param.22) | copy-start | bytes 1156
  0.7 6.5 %copy-start.10 = (bf16[48]{0:T(256)(128)(2,1)S(1)}, bf16[48]{0:T(256)(128)(2,1)}, u32[]{:S(2)}) copy-start(bf16[48]{0:T(256)(128)(2,1)} %param.21) | copy-start | bytes 292
  0.7 6.5 %copy-start.11 = (bf16[48]{0:T(256)(128)(2,1)S(1)}, bf16[48]{0:T(256)(128)(2,1)}, u32[]{:S(2)}) copy-start(bf16[48]{0:T(256)(128)(2,1)} %param.18) | copy-start | bytes 292
  0.7 6.6 %copy-start.6 = (bf16[48,3,384]{2,0,1:T(8,128)(2,1)S(1)}, bf16[48,3,384]{2,0,1:T(8,128)(2,1)}, u32[]{:S(2)}) copy-start(bf16[48,3,384]{2,0,1:T(8,128)(2,1)} %param.19) | copy-start | bytes 331780
  0.7 6.6 %copy-start.8 = (bf16[384,48]{0,1:T(8,128)(2,1)S(1)}, bf16[384,48]{0,1:T(8,128)(2,1)}, u32[]{:S(2)}) copy-start(bf16[384,48]{0,1:T(8,128)(2,1)} %param.20) | copy-start | bytes 110596
  2.8 5.2 %copy-start.5 = (bf16[48,2,1024]{2,1,0:T(2,128)(2,1)S(1)}, bf16[48,2,1024]{2,1,0:T(2,128)(2,1)}, u32[]{:S(2)}) copy-start(bf16[48,2,1024]{2,1,0:T(2,128)(2,1)} %param.25) | copy-start | bytes 589828
  2.9 5.1 %copy-start.7 = (bf16[1024,48]{0,1:T(8,128)(2,1)S(1)}, bf16[1024,48]{0,1:T(8,128)(2,1)}, u32[]{:S(2)}) copy-start(bf16[1024,48]{0,1:T(8,128)(2,1)} %param.26) | copy-start | bytes 294916
  4.5 4.2 %copy-start.1 = (bf16[4,48,2,1024]{3,2,1,0:T(2,128)(2,1)S(1)}, bf16[4,48,2,1024]{3,2,1,0:T(2,128)(2,1)}, u32[]{:S(2)}) copy-start(bf16[4,48,2,1024]{3,2,1,0:T(2,128)(2,1)} %param.23) | copy-start | bytes 2359300
  7.1 2.2 copy-start.3
  241.1 2.4 copy-start.4
  243.5 1.8 copy-start.2
  244.2 2.0 copy-start
